TPU v7x, 128 devices: a whole 4x4x4 slice. The times are simulated.
128 devices in a mesh: seq: 16 (over x_hi, y, core), head: 8 (over z, x_lo).
Axes of the slice: x: 4 (x_hi: 2, x_lo: 2; x = x_hi * 2 + x_lo), y: 4, z: 4, core: 2. Of those that a mesh axis runs over, the one named last changes fastest.
Arguments:
- query: bfloat16 [4096, 4096], P('seq', 'head'), may hold values from -30 to 30
- key_rows: bfloat16 [4096, 4096], P('seq', 'head'), may hold values from -4 to 4
- value_rows: bfloat16 [4096, 4096], P('seq', 'head'), may hold values from -6 to 6
- out_grad: bfloat16 [4096, 4096], P('seq', 'head'), may hold values from -6 to 6
- sample_blocks: int32 [3], replicated, may hold values from 1 to 20, as said below
Outputs:
- query_grad: bfloat16 [4096, 4096], P('seq', 'head')
- key_grad: bfloat16 [4096, 4096], P('seq', 'head')
- value_grad: bfloat16 [4096, 4096], P('seq', 'head')
Inputs may be any that keep to these rules, and one draw needn't show every extreme that they name: `sample_blocks`: the 3 samples lie one after another in the pack, each a whole number of 128-token blocks, together all 32 blocks; one sample has exactly 16 + max(1, 4) blocks.
All inputs are finite; a program needn't handle non-finite values.
Results may differ from a plain program's by a relative error of at most 0.005.
Values may be sent and summed in bfloat16 or wider, within the bound.
A program may use at most 64 MiB of HBM per device.

v0:
```python
import jax
import jax.numpy as jnp
from jax import lax
from jax.sharding import PartitionSpec as P

HD = 128
BLK = 128


masked_fill = -1e30


def passed_along(block, axis, distance):
    devices = range(lax.axis_size(axis))
    route = [((i - distance) % len(devices), i) for i in devices]
    return lax.ppermute(block, axis, route)


def segment_of(positions, sample_blocks):
    sample_ends = jnp.cumsum(sample_blocks)
    block_index = positions // BLK
    return jnp.sum((block_index[:, None] >= sample_ends[None, :]).astype(jnp.int32), axis=1)


def send_onward(key_grad, value_grad):
    return passed_along((key_grad, value_grad), "seq", 1)


def local(query, key_rows, value_rows, out_grad, sample_blocks):
    row_count = query.shape[0]
    head_count = query.shape[1] // HD
    scaling = HD ** (-0.5)
    seq_count = lax.axis_size("seq")
    seq_index = lax.axis_index("seq")
    query_seg = segment_of(
        seq_index * row_count + jnp.arange(row_count, dtype=jnp.int32), sample_blocks
    )
    query_heads = query.reshape(row_count, head_count, HD)
    grad_heads = out_grad.reshape(row_count, head_count, HD)

    def stats_step(carried, shard_pair, first_row):
        run_max, run_sum, run_dot = carried
        key_count = shard_pair[0].shape[0]
        key_seg = segment_of(first_row + jnp.arange(key_count, dtype=jnp.int32), sample_blocks)
        allowed = query_seg[:, None] == key_seg[None, :]
        key_heads = shard_pair[0].reshape(key_count, head_count, HD)
        value_heads = shard_pair[1].reshape(key_count, head_count, HD)
        scores = (
            jnp.einsum("qhd,khd->hqk", query_heads, key_heads, preferred_element_type=jnp.float32)
            * scaling
        )
        new_max = jnp.maximum(
            run_max, jnp.max(jnp.where(allowed[None], scores, masked_fill), axis=2)
        )
        exp_terms = jnp.where(allowed[None], jnp.exp(scores - new_max[:, :, None]), 0.0)
        prob_grad = jnp.einsum(
            "qhd,khd->hqk", grad_heads, value_heads, preferred_element_type=jnp.float32
        )
        factor = jnp.exp(run_max - new_max)
        return (
            new_max,
            run_sum * factor + jnp.sum(exp_terms, axis=2),
            run_dot * factor + jnp.sum(exp_terms * prob_grad, axis=2),
        )

    start_stats = (
        jnp.full((head_count, row_count), masked_fill, jnp.float32),
        jnp.zeros((head_count, row_count), jnp.float32),
        jnp.zeros((head_count, row_count), jnp.float32),
    )
    key_all, value_all = (
        lax.all_gather(key_rows, "seq", axis=0, tiled=True),
        lax.all_gather(value_rows, "seq", axis=0, tiled=True),
    )

    def stats_turn(anchor, carried):
        first_row = anchor * row_count
        key_piece = lax.dynamic_slice_in_dim(key_all, first_row, row_count, 0)
        value_piece = lax.dynamic_slice_in_dim(value_all, first_row, row_count, 0)
        return stats_step(carried, (key_piece, value_piece), first_row)

    row_max, row_sum, row_dot = lax.fori_loop(0, seq_count, stats_turn, start_stats)
    delta = row_dot / row_sum

    def pick(anchor, first_col, col_width):
        first_row = anchor * row_count
        key_piece = lax.dynamic_slice(key_all, (first_row, first_col), (row_count, col_width))
        value_piece = lax.dynamic_slice(value_all, (first_row, first_col), (row_count, col_width))
        return (key_piece, value_piece)

    def grads_of(first_head, head_width, key_block, value_block, anchor):
        key_block, value_block = pick(anchor, first_head * HD, head_width * HD)
        key_count = key_block.shape[0]
        last_head = first_head + head_width
        key_seg = segment_of(
            anchor * key_count + jnp.arange(key_count, dtype=jnp.int32), sample_blocks
        )
        allowed = query_seg[:, None] == key_seg[None, :]
        key_heads = key_block.reshape(key_count, head_width, HD)
        value_heads = value_block.reshape(key_count, head_width, HD)
        scores = (
            jnp.einsum("qhd,khd->hqk", query_heads, key_heads, preferred_element_type=jnp.float32)
            * scaling
        )
        probability = jnp.where(
            allowed[None],
            jnp.exp(scores - row_max[first_head:last_head, :, None])
            / row_sum[first_head:last_head, :, None],
            0.0,
        )
        prob_grad = jnp.einsum(
            "qhd,khd->hqk", grad_heads, value_heads, preferred_element_type=jnp.float32
        )
        score_grad = probability * (prob_grad - delta[first_head:last_head, :, None])
        score_low = score_grad.astype(jnp.bfloat16)
        prob_low = probability.astype(jnp.bfloat16)
        query_add = jnp.einsum(
            "hqk,khd->qhd", score_low, key_heads, preferred_element_type=jnp.float32
        )
        key_add = jnp.einsum(
            "hqk,qhd->khd", score_low, query_heads, preferred_element_type=jnp.float32
        )
        value_add = jnp.einsum(
            "hqk,qhd->khd", prob_low, grad_heads, preferred_element_type=jnp.float32
        )
        return (query_add, key_add, value_add)

    query_zero = jnp.zeros((row_count, head_count, HD), jnp.float32)

    def advance(turn_index, carried):
        key_block, value_block, query_acc, dkey_acc, dvalue_acc = carried
        added = grads_of(
            0, head_count, key_block, value_block, (seq_index - turn_index) % seq_count
        )
        dkey_acc, dvalue_acc = send_onward(dkey_acc + added[1], dvalue_acc + added[2])
        return (key_block, value_block, query_acc + added[0], dkey_acc, dvalue_acc)

    final = lax.fori_loop(
        0, seq_count - 1, advance, (key_rows, value_rows, query_zero, query_zero, query_zero)
    )
    added = grads_of(0, head_count, final[0], final[1], (seq_index - seq_count + 1) % seq_count)
    query_total = final[2] + added[0]
    key_total, value_total = send_onward(final[3] + added[1], final[4] + added[2])
    query_grad = (scaling * query_total).reshape(row_count, head_count * HD).astype(jnp.bfloat16)
    key_grad = (scaling * key_total).reshape(row_count, head_count * HD).astype(jnp.bfloat16)
    value_grad = value_total.reshape(row_count, head_count * HD).astype(jnp.bfloat16)
    return (query_grad, key_grad, value_grad)


def solution(mesh):
    in_specs = (P("seq", "head"), P("seq", "head"), P("seq", "head"), P("seq", "head"), P())
    out_specs = (P("seq", "head"), P("seq", "head"), P("seq", "head"))
    return jax.shard_map(local, mesh=mesh, in_specs=in_specs, out_specs=out_specs, check_vma=False)
```

profile of v0, /device:TPU:0, one launch (start us, length us, event | category | flops | bytes accessed | tf_op | source)
XLA Modules:
  0.0 526.1 jit_solution(16354416388930692596)
XLA Ops:
  7.2 1.8 copy.47
  9.1 1.8 copy.49
  14.5 55.4 %all-gather.3.cloned.1.call-done = bf16[4096,512]{0,1:T(8,128)(2,1)} async-done(((bf16[256,512]{0,1:T(8,128)(2,1)}), bf16[4096,512]{0,1:T(8,128)(2,1)}) %all-gather.3.cloned.1.call-update) | async-done | bytes 4194320 | tf_op jit(solution)/shard_map/all_gather | solution.py:72
  69.9 57.2 %all-gather.5.cloned.1.call-done = bf16[4096,512]{0,1:T(8,128)(2,1)} async-done(((bf16[256,512]{0,1:T(8,128)(2,1)}), bf16[4096,512]{0,1:T(8,128)(2,1)}) %all-gather.5.cloned.1.call-update) | async-done | bytes 4194320 | tf_op jit(solution)/shard_map/all_gather | solution.py:73
  127.2 38.2 %while.40 = (s32[]{:T(128)}, f32[4,256]{1,0:T(4,128)S(1)}, f32[4,256]{1,0:T(4,128)S(1)}, f32[4,256]{1,0:T(4,128)S(1)}, s32[256]{0:T(256)S(1)}, /*index=5*/s32[1,...) while((s32[]{:T(128)}, f32[4,256]{1,0:T(4,128)S(1)}, ...), condition=%wide.region_7.8_spmd.clone, body=%wide.region_2.7_spmd.clone.sunk | while | flops 136918016 | bytes 5584090 | solution.py:82
  165.5 332.5 %while.41 = (s32[]{:T(128)}, f32[256,4,128]{0,2,1:T(8,128)S(1)}, f32[256,4,128]{2,0,1:T(8,128)S(1)}, f32[256,4,128]{2,0,1:T(8,128)S(1)}, s32[]{:T(128)}, /*index...) while((s32[]{:T(128)}, f32[256,4,128]{0,2,1:T(8,128)S(1)}, ...), condition=%wide.region_10.11_spmd.clone, body=%wide.region_8.10_spmd.clone.sunk | while | flops 338237440 | bytes 15091150 | solution.py:138
  170.0 1.2 fusion.97
  171.4 10.7 %collective-permute-done = f32[256,4,128]{2,0,1:T(8,128)S(1)} collective-permute-done((f32[256,4,128]{2,0,1:T(8,128)}, f32[256,4,128]{2,0,1:T(8,128)S(1)}, u32[]{:S(2)}, u32[]{:S(2)}) %collective-permute-start) | collective-permute-done | bytes 524320 | tf_op jit(solution)/shard_map/while/body/eval_jaxpr/ppermute | solution.py:16
  182.1 5.6 %collective-permute-done.1 = f32[256,4,128]{2,0,1:T(8,128)S(1)} collective-permute-done((f32[256,4,128]{2,0,1:T(8,128)}, f32[256,4,128]{2,0,1:T(8,128)S(1)}, u32[]{:S(2)}, u32[]{:S(2)}) %collective-permute-start.1) | collective-permute-done | bytes 524320 | tf_op jit(solution)/shard_map/while/body/eval_jaxpr/ppermute | solution.py:16
  191.8 1.2 fusion.97
  193.3 11.0 %collective-permute-done = f32[256,4,128]{2,0,1:T(8,128)S(1)} collective-permute-done((f32[256,4,128]{2,0,1:T(8,128)}, f32[256,4,128]{2,0,1:T(8,128)S(1)}, u32[]{:S(2)}, u32[]{:S(2)}) %collective-permute-start) | collective-permute-done | bytes 524320 | tf_op jit(solution)/shard_map/while/body/eval_jaxpr/ppermute | solution.py:16
  204.3 5.6 %collective-permute-done.1 = f32[256,4,128]{2,0,1:T(8,128)S(1)} collective-permute-done((f32[256,4,128]{2,0,1:T(8,128)}, f32[256,4,128]{2,0,1:T(8,128)S(1)}, u32[]{:S(2)}, u32[]{:S(2)}) %collective-permute-start.1) | collective-permute-done | bytes 524320 | tf_op jit(solution)/shard_map/while/body/eval_jaxpr/ppermute | solution.py:16
  214.0 1.2 fusion.97
  215.4 11.0 %collective-permute-done = f32[256,4,128]{2,0,1:T(8,128)S(1)} collective-permute-done((f32[256,4,128]{2,0,1:T(8,128)}, f32[256,4,128]{2,0,1:T(8,128)S(1)}, u32[]{:S(2)}, u32[]{:S(2)}) %collective-permute-start) | collective-permute-done | bytes 524320 | tf_op jit(solution)/shard_map/while/body/eval_jaxpr/ppermute | solution.py:16
  226.4 5.6 %collective-permute-done.1 = f32[256,4,128]{2,0,1:T(8,128)S(1)} collective-permute-done((f32[256,4,128]{2,0,1:T(8,128)}, f32[256,4,128]{2,0,1:T(8,128)S(1)}, u32[]{:S(2)}, u32[]{:S(2)}) %collective-permute-start.1) | collective-permute-done | bytes 524320 | tf_op jit(solution)/shard_map/while/body/eval_jaxpr/ppermute | solution.py:16
  236.2 1.2 fusion.97
  237.6 11.0 %collective-permute-done = f32[256,4,128]{2,0,1:T(8,128)S(1)} collective-permute-done((f32[256,4,128]{2,0,1:T(8,128)}, f32[256,4,128]{2,0,1:T(8,128)S(1)}, u32[]{:S(2)}, u32[]{:S(2)}) %collective-permute-start) | collective-permute-done | bytes 524320 | tf_op jit(solution)/shard_map/while/body/eval_jaxpr/ppermute | solution.py:16
  248.6 5.6 %collective-permute-done.1 = f32[256,4,128]{2,0,1:T(8,128)S(1)} collective-permute-done((f32[256,4,128]{2,0,1:T(8,128)}, f32[256,4,128]{2,0,1:T(8,128)S(1)}, u32[]{:S(2)}, u32[]{:S(2)}) %collective-permute-start.1) | collective-permute-done | bytes 524320 | tf_op jit(solution)/shard_map/while/body/eval_jaxpr/ppermute | solution.py:16
  258.3 1.2 fusion.97
  259.8 11.0 %collective-permute-done = f32[256,4,128]{2,0,1:T(8,128)S(1)} collective-permute-done((f32[256,4,128]{2,0,1:T(8,128)}, f32[256,4,128]{2,0,1:T(8,128)S(1)}, u32[]{:S(2)}, u32[]{:S(2)}) %collective-permute-start) | collective-permute-done | bytes 524320 | tf_op jit(solution)/shard_map/while/body/eval_jaxpr/ppermute | solution.py:16
  270.8 5.6 %collective-permute-done.1 = f32[256,4,128]{2,0,1:T(8,128)S(1)} collective-permute-done((f32[256,4,128]{2,0,1:T(8,128)}, f32[256,4,128]{2,0,1:T(8,128)S(1)}, u32[]{:S(2)}, u32[]{:S(2)}) %collective-permute-start.1) | collective-permute-done | bytes 524320 | tf_op jit(solution)/shard_map/while/body/eval_jaxpr/ppermute | solution.py:16
  280.5 1.2 fusion.97
  281.9 11.0 %collective-permute-done = f32[256,4,128]{2,0,1:T(8,128)S(1)} collective-permute-done((f32[256,4,128]{2,0,1:T(8,128)}, f32[256,4,128]{2,0,1:T(8,128)S(1)}, u32[]{:S(2)}, u32[]{:S(2)}) %collective-permute-start) | collective-permute-done | bytes 524320 | tf_op jit(solution)/shard_map/while/body/eval_jaxpr/ppermute | solution.py:16
  292.9 5.6 %collective-permute-done.1 = f32[256,4,128]{2,0,1:T(8,128)S(1)} collective-permute-done((f32[256,4,128]{2,0,1:T(8,128)}, f32[256,4,128]{2,0,1:T(8,128)S(1)}, u32[]{:S(2)}, u32[]{:S(2)}) %collective-permute-start.1) | collective-permute-done | bytes 524320 | tf_op jit(solution)/shard_map/while/body/eval_jaxpr/ppermute | solution.py:16
  302.7 1.2 fusion.97
  304.1 11.0 %collective-permute-done = f32[256,4,128]{2,0,1:T(8,128)S(1)} collective-permute-done((f32[256,4,128]{2,0,1:T(8,128)}, f32[256,4,128]{2,0,1:T(8,128)S(1)}, u32[]{:S(2)}, u32[]{:S(2)}) %collective-permute-start) | collective-permute-done | bytes 524320 | tf_op jit(solution)/shard_map/while/body/eval_jaxpr/ppermute | solution.py:16
  315.1 5.6 %collective-permute-done.1 = f32[256,4,128]{2,0,1:T(8,128)S(1)} collective-permute-done((f32[256,4,128]{2,0,1:T(8,128)}, f32[256,4,128]{2,0,1:T(8,128)S(1)}, u32[]{:S(2)}, u32[]{:S(2)}) %collective-permute-start.1) | collective-permute-done | bytes 524320 | tf_op jit(solution)/shard_map/while/body/eval_jaxpr/ppermute | solution.py:16
  324.8 1.2 fusion.97
  326.2 11.0 %collective-permute-done = f32[256,4,128]{2,0,1:T(8,128)S(1)} collective-permute-done((f32[256,4,128]{2,0,1:T(8,128)}, f32[256,4,128]{2,0,1:T(8,128)S(1)}, u32[]{:S(2)}, u32[]{:S(2)}) %collective-permute-start) | collective-permute-done | bytes 524320 | tf_op jit(solution)/shard_map/while/body/eval_jaxpr/ppermute | solution.py:16
  337.2 5.6 %collective-permute-done.1 = f32[256,4,128]{2,0,1:T(8,128)S(1)} collective-permute-done((f32[256,4,128]{2,0,1:T(8,128)}, f32[256,4,128]{2,0,1:T(8,128)S(1)}, u32[]{:S(2)}, u32[]{:S(2)}) %collective-permute-start.1) | collective-permute-done | bytes 524320 | tf_op jit(solution)/shard_map/while/body/eval_jaxpr/ppermute | solution.py:16
  347.0 1.2 fusion.97
  348.4 11.0 %collective-permute-done = f32[256,4,128]{2,0,1:T(8,128)S(1)} collective-permute-done((f32[256,4,128]{2,0,1:T(8,128)}, f32[256,4,128]{2,0,1:T(8,128)S(1)}, u32[]{:S(2)}, u32[]{:S(2)}) %collective-permute-start) | collective-permute-done | bytes 524320 | tf_op jit(solution)/shard_map/while/body/eval_jaxpr/ppermute | solution.py:16
  359.4 5.6 %collective-permute-done.1 = f32[256,4,128]{2,0,1:T(8,128)S(1)} collective-permute-done((f32[256,4,128]{2,0,1:T(8,128)}, f32[256,4,128]{2,0,1:T(8,128)S(1)}, u32[]{:S(2)}, u32[]{:S(2)}) %collective-permute-start.1) | collective-permute-done | bytes 524320 | tf_op jit(solution)/shard_map/while/body/eval_jaxpr/ppermute | solution.py:16
  370.6 11.0 %collective-permute-done = f32[256,4,128]{2,0,1:T(8,128)S(1)} collective-permute-done((f32[256,4,128]{2,0,1:T(8,128)}, f32[256,4,128]{2,0,1:T(8,128)S(1)}, u32[]{:S(2)}, u32[]{:S(2)}) %collective-permute-start) | collective-permute-done | bytes 524320 | tf_op jit(solution)/shard_map/while/body/eval_jaxpr/ppermute | solution.py:16
  381.6 5.6 %collective-permute-done.1 = f32[256,4,128]{2,0,1:T(8,128)S(1)} collective-permute-done((f32[256,4,128]{2,0,1:T(8,128)}, f32[256,4,128]{2,0,1:T(8,128)S(1)}, u32[]{:S(2)}, u32[]{:S(2)}) %collective-permute-start.1) | collective-permute-done | bytes 524320 | tf_op jit(solution)/shard_map/while/body/eval_jaxpr/ppermute | solution.py:16
  391.3 1.2 fusion.97
  392.7 11.0 %collective-permute-done = f32[256,4,128]{2,0,1:T(8,128)S(1)} collective-permute-done((f32[256,4,128]{2,0,1:T(8,128)}, f32[256,4,128]{2,0,1:T(8,128)S(1)}, u32[]{:S(2)}, u32[]{:S(2)}) %collective-permute-start) | collective-permute-done | bytes 524320 | tf_op jit(solution)/shard_map/while/body/eval_jaxpr/ppermute | solution.py:16
  403.7 5.6 %collective-permute-done.1 = f32[256,4,128]{2,0,1:T(8,128)S(1)} collective-permute-done((f32[256,4,128]{2,0,1:T(8,128)}, f32[256,4,128]{2,0,1:T(8,128)S(1)}, u32[]{:S(2)}, u32[]{:S(2)}) %collective-permute-start.1) | collective-permute-done | bytes 524320 | tf_op jit(solution)/shard_map/while/body/eval_jaxpr/ppermute | solution.py:16
  414.9 11.0 %collective-permute-done = f32[256,4,128]{2,0,1:T(8,128)S(1)} collective-permute-done((f32[256,4,128]{2,0,1:T(8,128)}, f32[256,4,128]{2,0,1:T(8,128)S(1)}, u32[]{:S(2)}, u32[]{:S(2)}) %collective-permute-start) | collective-permute-done | bytes 524320 | tf_op jit(solution)/shard_map/while/body/eval_jaxpr/ppermute | solution.py:16
  425.9 5.6 %collective-permute-done.1 = f32[256,4,128]{2,0,1:T(8,128)S(1)} collective-permute-done((f32[256,4,128]{2,0,1:T(8,128)}, f32[256,4,128]{2,0,1:T(8,128)S(1)}, u32[]{:S(2)}, u32[]{:S(2)}) %collective-permute-start.1) | collective-permute-done | bytes 524320 | tf_op jit(solution)/shard_map/while/body/eval_jaxpr/ppermute | solution.py:16
  435.6 1.2 fusion.97
  437.1 11.0 %collective-permute-done = f32[256,4,128]{2,0,1:T(8,128)S(1)} collective-permute-done((f32[256,4,128]{2,0,1:T(8,128)}, f32[256,4,128]{2,0,1:T(8,128)S(1)}, u32[]{:S(2)}, u32[]{:S(2)}) %collective-permute-start) | collective-permute-done | bytes 524320 | tf_op jit(solution)/shard_map/while/body/eval_jaxpr/ppermute | solution.py:16
  448.1 5.6 %collective-permute-done.1 = f32[256,4,128]{2,0,1:T(8,128)S(1)} collective-permute-done((f32[256,4,128]{2,0,1:T(8,128)}, f32[256,4,128]{2,0,1:T(8,128)S(1)}, u32[]{:S(2)}, u32[]{:S(2)}) %collective-permute-start.1) | collective-permute-done | bytes 524320 | tf_op jit(solution)/shard_map/while/body/eval_jaxpr/ppermute | solution.py:16
  459.2 11.0 %collective-permute-done = f32[256,4,128]{2,0,1:T(8,128)S(1)} collective-permute-done((f32[256,4,128]{2,0,1:T(8,128)}, f32[256,4,128]{2,0,1:T(8,128)S(1)}, u32[]{:S(2)}, u32[]{:S(2)}) %collective-permute-start) | collective-permute-done | bytes 524320 | tf_op jit(solution)/shard_map/while/body/eval_jaxpr/ppermute | solution.py:16
  470.2 5.6 %collective-permute-done.1 = f32[256,4,128]{2,0,1:T(8,128)S(1)} collective-permute-done((f32[256,4,128]{2,0,1:T(8,128)}, f32[256,4,128]{2,0,1:T(8,128)S(1)}, u32[]{:S(2)}, u32[]{:S(2)}) %collective-permute-start.1) | collective-permute-done | bytes 524320 | tf_op jit(solution)/shard_map/while/body/eval_jaxpr/ppermute | solution.py:16
  481.4 11.0 %collective-permute-done = f32[256,4,128]{2,0,1:T(8,128)S(1)} collective-permute-done((f32[256,4,128]{2,0,1:T(8,128)}, f32[256,4,128]{2,0,1:T(8,128)S(1)}, u32[]{:S(2)}, u32[]{:S(2)}) %collective-permute-start) | collective-permute-done | bytes 524320 | tf_op jit(solution)/shard_map/while/body/eval_jaxpr/ppermute | solution.py:16
  492.4 5.6 %collective-permute-done.1 = f32[256,4,128]{2,0,1:T(8,128)S(1)} collective-permute-done((f32[256,4,128]{2,0,1:T(8,128)}, f32[256,4,128]{2,0,1:T(8,128)S(1)}, u32[]{:S(2)}, u32[]{:S(2)}) %collective-permute-start.1) | collective-permute-done | bytes 524320 | tf_op jit(solution)/shard_map/while/body/eval_jaxpr/ppermute | solution.py:16
  503.6 13.8 %collective-permute-done.3 = bf16[256,4,128]{2,0,1:T(8,128)(2,1)S(1)} collective-permute-done((bf16[256,4,128]{2,0,1:T(8,128)(2,1)S(1)}, bf16[256,4,128]{2,0,1:T(8,128)(2,1)S(1)}, u32[]{:S(2)}, u32[]{:S(2)}) %collective-permute-start.3) | collective-permute-done | bytes 262176 | tf_op jit(solution)/shard_map/ppermute | solution.py:16
  (364 shorter events, 118.3 us)
Async XLA Ops:
  7.2 62.8 %all-gather.3.cloned.1.call-start = ((), (), s32[]{:S(2)}) async-start(), calls=%async_computation | async-start | bytes 4456448 | tf_op jit(solution)/shard_map/all_gather | solution.py:72
  9.0 118.1 %all-gather.5.cloned.1.call-start = ((), (), s32[]{:S(2)}) async-start(), calls=%async_computation.1 | async-start | bytes 4456448 | tf_op jit(solution)/shard_map/all_gather | solution.py:73
  169.7 12.4 %collective-permute-start = (f32[256,4,128]{2,0,1:T(8,128)}, f32[256,4,128]{2,0,1:T(8,128)S(1)}, u32[]{:S(2)}, u32[]{:S(2)}) collective-permute-start(f32[256,4,128]{2,0,1:T(8,128)} %fusion.96), channel_id=1, source_target_pairs={{120,0},{0,8},{8,16},{16,24},{24,32},{32,40},{40,48},{48,56},{56,6... | collective-permute-start | bytes 1572872 | tf_op jit(solution)/shard_map/while/body/eval_jaxpr/ppermute | solution.py:16
  171.1 16.6 %collective-permute-start.1 = (f32[256,4,128]{2,0,1:T(8,128)}, f32[256,4,128]{2,0,1:T(8,128)S(1)}, u32[]{:S(2)}, u32[]{:S(2)}) collective-permute-start(f32[256,4,128]{2,0,1:T(8,128)} %fusion.97), channel_id=1, source_target_pairs={{120,0},{0,8},{8,16},{16,24},{24,32},{32,40},{40,48},{48,56},{56,6... | collective-permute-start | bytes 1572872 | tf_op jit(solution)/shard_map/while/body/eval_jaxpr/ppermute | solution.py:16
  191.8 12.4 %collective-permute-start = (f32[256,4,128]{2,0,1:T(8,128)}, f32[256,4,128]{2,0,1:T(8,128)S(1)}, u32[]{:S(2)}, u32[]{:S(2)}) collective-permute-start(f32[256,4,128]{2,0,1:T(8,128)} %fusion.96), channel_id=1, source_target_pairs={{120,0},{0,8},{8,16},{16,24},{24,32},{32,40},{40,48},{48,56},{56,6... | collective-permute-start | bytes 1572872 | tf_op jit(solution)/shard_map/while/body/eval_jaxpr/ppermute | solution.py:16
  193.0 16.9 %collective-permute-start.1 = (f32[256,4,128]{2,0,1:T(8,128)}, f32[256,4,128]{2,0,1:T(8,128)S(1)}, u32[]{:S(2)}, u32[]{:S(2)}) collective-permute-start(f32[256,4,128]{2,0,1:T(8,128)} %fusion.97), channel_id=1, source_target_pairs={{120,0},{0,8},{8,16},{16,24},{24,32},{32,40},{40,48},{48,56},{56,6... | collective-permute-start | bytes 1572872 | tf_op jit(solution)/shard_map/while/body/eval_jaxpr/ppermute | solution.py:16
  214.0 12.4 %collective-permute-start = (f32[256,4,128]{2,0,1:T(8,128)}, f32[256,4,128]{2,0,1:T(8,128)S(1)}, u32[]{:S(2)}, u32[]{:S(2)}) collective-permute-start(f32[256,4,128]{2,0,1:T(8,128)} %fusion.96), channel_id=1, source_target_pairs={{120,0},{0,8},{8,16},{16,24},{24,32},{32,40},{40,48},{48,56},{56,6... | collective-permute-start | bytes 1572872 | tf_op jit(solution)/shard_map/while/body/eval_jaxpr/ppermute | solution.py:16
  215.2 16.9 %collective-permute-start.1 = (f32[256,4,128]{2,0,1:T(8,128)}, f32[256,4,128]{2,0,1:T(8,128)S(1)}, u32[]{:S(2)}, u32[]{:S(2)}) collective-permute-start(f32[256,4,128]{2,0,1:T(8,128)} %fusion.97), channel_id=1, source_target_pairs={{120,0},{0,8},{8,16},{16,24},{24,32},{32,40},{40,48},{48,56},{56,6... | collective-permute-start | bytes 1572872 | tf_op jit(solution)/shard_map/while/body/eval_jaxpr/ppermute | solution.py:16
  236.2 12.4 %collective-permute-start = (f32[256,4,128]{2,0,1:T(8,128)}, f32[256,4,128]{2,0,1:T(8,128)S(1)}, u32[]{:S(2)}, u32[]{:S(2)}) collective-permute-start(f32[256,4,128]{2,0,1:T(8,128)} %fusion.96), channel_id=1, source_target_pairs={{120,0},{0,8},{8,16},{16,24},{24,32},{32,40},{40,48},{48,56},{56,6... | collective-permute-start | bytes 1572872 | tf_op jit(solution)/shard_map/while/body/eval_jaxpr/ppermute | solution.py:16
  237.3 16.9 %collective-permute-start.1 = (f32[256,4,128]{2,0,1:T(8,128)}, f32[256,4,128]{2,0,1:T(8,128)S(1)}, u32[]{:S(2)}, u32[]{:S(2)}) collective-permute-start(f32[256,4,128]{2,0,1:T(8,128)} %fusion.97), channel_id=1, source_target_pairs={{120,0},{0,8},{8,16},{16,24},{24,32},{32,40},{40,48},{48,56},{56,6... | collective-permute-start | bytes 1572872 | tf_op jit(solution)/shard_map/while/body/eval_jaxpr/ppermute | solution.py:16
  258.3 12.4 %collective-permute-start = (f32[256,4,128]{2,0,1:T(8,128)}, f32[256,4,128]{2,0,1:T(8,128)S(1)}, u32[]{:S(2)}, u32[]{:S(2)}) collective-permute-start(f32[256,4,128]{2,0,1:T(8,128)} %fusion.96), channel_id=1, source_target_pairs={{120,0},{0,8},{8,16},{16,24},{24,32},{32,40},{40,48},{48,56},{56,6... | collective-permute-start | bytes 1572872 | tf_op jit(solution)/shard_map/while/body/eval_jaxpr/ppermute | solution.py:16
  259.5 16.9 %collective-permute-start.1 = (f32[256,4,128]{2,0,1:T(8,128)}, f32[256,4,128]{2,0,1:T(8,128)S(1)}, u32[]{:S(2)}, u32[]{:S(2)}) collective-permute-start(f32[256,4,128]{2,0,1:T(8,128)} %fusion.97), channel_id=1, source_target_pairs={{120,0},{0,8},{8,16},{16,24},{24,32},{32,40},{40,48},{48,56},{56,6... | collective-permute-start | bytes 1572872 | tf_op jit(solution)/shard_map/while/body/eval_jaxpr/ppermute | solution.py:16
  280.5 12.4 %collective-permute-start = (f32[256,4,128]{2,0,1:T(8,128)}, f32[256,4,128]{2,0,1:T(8,128)S(1)}, u32[]{:S(2)}, u32[]{:S(2)}) collective-permute-start(f32[256,4,128]{2,0,1:T(8,128)} %fusion.96), channel_id=1, source_target_pairs={{120,0},{0,8},{8,16},{16,24},{24,32},{32,40},{40,48},{48,56},{56,6... | collective-permute-start | bytes 1572872 | tf_op jit(solution)/shard_map/while/body/eval_jaxpr/ppermute | solution.py:16
  281.6 16.9 %collective-permute-start.1 = (f32[256,4,128]{2,0,1:T(8,128)}, f32[256,4,128]{2,0,1:T(8,128)S(1)}, u32[]{:S(2)}, u32[]{:S(2)}) collective-permute-start(f32[256,4,128]{2,0,1:T(8,128)} %fusion.97), channel_id=1, source_target_pairs={{120,0},{0,8},{8,16},{16,24},{24,32},{32,40},{40,48},{48,56},{56,6... | collective-permute-start | bytes 1572872 | tf_op jit(solution)/shard_map/while/body/eval_jaxpr/ppermute | solution.py:16
  302.7 12.4 %collective-permute-start = (f32[256,4,128]{2,0,1:T(8,128)}, f32[256,4,128]{2,0,1:T(8,128)S(1)}, u32[]{:S(2)}, u32[]{:S(2)}) collective-permute-start(f32[256,4,128]{2,0,1:T(8,128)} %fusion.96), channel_id=1, source_target_pairs={{120,0},{0,8},{8,16},{16,24},{24,32},{32,40},{40,48},{48,56},{56,6... | collective-permute-start | bytes 1572872 | tf_op jit(solution)/shard_map/while/body/eval_jaxpr/ppermute | solution.py:16
  303.8 16.9 %collective-permute-start.1 = (f32[256,4,128]{2,0,1:T(8,128)}, f32[256,4,128]{2,0,1:T(8,128)S(1)}, u32[]{:S(2)}, u32[]{:S(2)}) collective-permute-start(f32[256,4,128]{2,0,1:T(8,128)} %fusion.97), channel_id=1, source_target_pairs={{120,0},{0,8},{8,16},{16,24},{24,32},{32,40},{40,48},{48,56},{56,6... | collective-permute-start | bytes 1572872 | tf_op jit(solution)/shard_map/while/body/eval_jaxpr/ppermute | solution.py:16
  324.8 12.4 %collective-permute-start = (f32[256,4,128]{2,0,1:T(8,128)}, f32[256,4,128]{2,0,1:T(8,128)S(1)}, u32[]{:S(2)}, u32[]{:S(2)}) collective-permute-start(f32[256,4,128]{2,0,1:T(8,128)} %fusion.96), channel_id=1, source_target_pairs={{120,0},{0,8},{8,16},{16,24},{24,32},{32,40},{40,48},{48,56},{56,6... | collective-permute-start | bytes 1572872 | tf_op jit(solution)/shard_map/while/body/eval_jaxpr/ppermute | solution.py:16
  326.0 16.9 %collective-permute-start.1 = (f32[256,4,128]{2,0,1:T(8,128)}, f32[256,4,128]{2,0,1:T(8,128)S(1)}, u32[]{:S(2)}, u32[]{:S(2)}) collective-permute-start(f32[256,4,128]{2,0,1:T(8,128)} %fusion.97), channel_id=1, source_target_pairs={{120,0},{0,8},{8,16},{16,24},{24,32},{32,40},{40,48},{48,56},{56,6... | collective-permute-start | bytes 1572872 | tf_op jit(solution)/shard_map/while/body/eval_jaxpr/ppermute | solution.py:16
  347.0 12.4 %collective-permute-start = (f32[256,4,128]{2,0,1:T(8,128)}, f32[256,4,128]{2,0,1:T(8,128)S(1)}, u32[]{:S(2)}, u32[]{:S(2)}) collective-permute-start(f32[256,4,128]{2,0,1:T(8,128)} %fusion.96), channel_id=1, source_target_pairs={{120,0},{0,8},{8,16},{16,24},{24,32},{32,40},{40,48},{48,56},{56,6... | collective-permute-start | bytes 1572872 | tf_op jit(solution)/shard_map/while/body/eval_jaxpr/ppermute | solution.py:16
  348.1 16.9 %collective-permute-start.1 = (f32[256,4,128]{2,0,1:T(8,128)}, f32[256,4,128]{2,0,1:T(8,128)S(1)}, u32[]{:S(2)}, u32[]{:S(2)}) collective-permute-start(f32[256,4,128]{2,0,1:T(8,128)} %fusion.97), channel_id=1, source_target_pairs={{120,0},{0,8},{8,16},{16,24},{24,32},{32,40},{40,48},{48,56},{56,6... | collective-permute-start | bytes 1572872 | tf_op jit(solution)/shard_map/while/body/eval_jaxpr/ppermute | solution.py:16
  369.1 12.4 %collective-permute-start = (f32[256,4,128]{2,0,1:T(8,128)}, f32[256,4,128]{2,0,1:T(8,128)S(1)}, u32[]{:S(2)}, u32[]{:S(2)}) collective-permute-start(f32[256,4,128]{2,0,1:T(8,128)} %fusion.96), channel_id=1, source_target_pairs={{120,0},{0,8},{8,16},{16,24},{24,32},{32,40},{40,48},{48,56},{56,6... | collective-permute-start | bytes 1572872 | tf_op jit(solution)/shard_map/while/body/eval_jaxpr/ppermute | solution.py:16
  370.3 16.9 %collective-permute-start.1 = (f32[256,4,128]{2,0,1:T(8,128)}, f32[256,4,128]{2,0,1:T(8,128)S(1)}, u32[]{:S(2)}, u32[]{:S(2)}) collective-permute-start(f32[256,4,128]{2,0,1:T(8,128)} %fusion.97), channel_id=1, source_target_pairs={{120,0},{0,8},{8,16},{16,24},{24,32},{32,40},{40,48},{48,56},{56,6... | collective-permute-start | bytes 1572872 | tf_op jit(solution)/shard_map/while/body/eval_jaxpr/ppermute | solution.py:16
  391.3 12.4 %collective-permute-start = (f32[256,4,128]{2,0,1:T(8,128)}, f32[256,4,128]{2,0,1:T(8,128)S(1)}, u32[]{:S(2)}, u32[]{:S(2)}) collective-permute-start(f32[256,4,128]{2,0,1:T(8,128)} %fusion.96), channel_id=1, source_target_pairs={{120,0},{0,8},{8,16},{16,24},{24,32},{32,40},{40,48},{48,56},{56,6... | collective-permute-start | bytes 1572872 | tf_op jit(solution)/shard_map/while/body/eval_jaxpr/ppermute | solution.py:16
  392.5 16.9 %collective-permute-start.1 = (f32[256,4,128]{2,0,1:T(8,128)}, f32[256,4,128]{2,0,1:T(8,128)S(1)}, u32[]{:S(2)}, u32[]{:S(2)}) collective-permute-start(f32[256,4,128]{2,0,1:T(8,128)} %fusion.97), channel_id=1, source_target_pairs={{120,0},{0,8},{8,16},{16,24},{24,32},{32,40},{40,48},{48,56},{56,6... | collective-permute-start | bytes 1572872 | tf_op jit(solution)/shard_map/while/body/eval_jaxpr/ppermute | solution.py:16
  413.5 12.4 %collective-permute-start = (f32[256,4,128]{2,0,1:T(8,128)}, f32[256,4,128]{2,0,1:T(8,128)S(1)}, u32[]{:S(2)}, u32[]{:S(2)}) collective-permute-start(f32[256,4,128]{2,0,1:T(8,128)} %fusion.96), channel_id=1, source_target_pairs={{120,0},{0,8},{8,16},{16,24},{24,32},{32,40},{40,48},{48,56},{56,6... | collective-permute-start | bytes 1572872 | tf_op jit(solution)/shard_map/while/body/eval_jaxpr/ppermute | solution.py:16
  414.6 16.9 %collective-permute-start.1 = (f32[256,4,128]{2,0,1:T(8,128)}, f32[256,4,128]{2,0,1:T(8,128)S(1)}, u32[]{:S(2)}, u32[]{:S(2)}) collective-permute-start(f32[256,4,128]{2,0,1:T(8,128)} %fusion.97), channel_id=1, source_target_pairs={{120,0},{0,8},{8,16},{16,24},{24,32},{32,40},{40,48},{48,56},{56,6... | collective-permute-start | bytes 1572872 | tf_op jit(solution)/shard_map/while/body/eval_jaxpr/ppermute | solution.py:16
  435.6 12.4 %collective-permute-start = (f32[256,4,128]{2,0,1:T(8,128)}, f32[256,4,128]{2,0,1:T(8,128)S(1)}, u32[]{:S(2)}, u32[]{:S(2)}) collective-permute-start(f32[256,4,128]{2,0,1:T(8,128)} %fusion.96), channel_id=1, source_target_pairs={{120,0},{0,8},{8,16},{16,24},{24,32},{32,40},{40,48},{48,56},{56,6... | collective-permute-start | bytes 1572872 | tf_op jit(solution)/shard_map/while/body/eval_jaxpr/ppermute | solution.py:16
  436.8 16.9 %collective-permute-start.1 = (f32[256,4,128]{2,0,1:T(8,128)}, f32[256,4,128]{2,0,1:T(8,128)S(1)}, u32[]{:S(2)}, u32[]{:S(2)}) collective-permute-start(f32[256,4,128]{2,0,1:T(8,128)} %fusion.97), channel_id=1, source_target_pairs={{120,0},{0,8},{8,16},{16,24},{24,32},{32,40},{40,48},{48,56},{56,6... | collective-permute-start | bytes 1572872 | tf_op jit(solution)/shard_map/while/body/eval_jaxpr/ppermute | solution.py:16
  457.8 12.4 %collective-permute-start = (f32[256,4,128]{2,0,1:T(8,128)}, f32[256,4,128]{2,0,1:T(8,128)S(1)}, u32[]{:S(2)}, u32[]{:S(2)}) collective-permute-start(f32[256,4,128]{2,0,1:T(8,128)} %fusion.96), channel_id=1, source_target_pairs={{120,0},{0,8},{8,16},{16,24},{24,32},{32,40},{40,48},{48,56},{56,6... | collective-permute-start | bytes 1572872 | tf_op jit(solution)/shard_map/while/body/eval_jaxpr/ppermute | solution.py:16
  459.0 16.9 %collective-permute-start.1 = (f32[256,4,128]{2,0,1:T(8,128)}, f32[256,4,128]{2,0,1:T(8,128)S(1)}, u32[]{:S(2)}, u32[]{:S(2)}) collective-permute-start(f32[256,4,128]{2,0,1:T(8,128)} %fusion.97), channel_id=1, source_target_pairs={{120,0},{0,8},{8,16},{16,24},{24,32},{32,40},{40,48},{48,56},{56,6... | collective-permute-start | bytes 1572872 | tf_op jit(solution)/shard_map/while/body/eval_jaxpr/ppermute | solution.py:16
  480.0 12.4 %collective-permute-start = (f32[256,4,128]{2,0,1:T(8,128)}, f32[256,4,128]{2,0,1:T(8,128)S(1)}, u32[]{:S(2)}, u32[]{:S(2)}) collective-permute-start(f32[256,4,128]{2,0,1:T(8,128)} %fusion.96), channel_id=1, source_target_pairs={{120,0},{0,8},{8,16},{16,24},{24,32},{32,40},{40,48},{48,56},{56,6... | collective-permute-start | bytes 1572872 | tf_op jit(solution)/shard_map/while/body/eval_jaxpr/ppermute | solution.py:16
  481.1 16.9 %collective-permute-start.1 = (f32[256,4,128]{2,0,1:T(8,128)}, f32[256,4,128]{2,0,1:T(8,128)S(1)}, u32[]{:S(2)}, u32[]{:S(2)}) collective-permute-start(f32[256,4,128]{2,0,1:T(8,128)} %fusion.97), channel_id=1, source_target_pairs={{120,0},{0,8},{8,16},{16,24},{24,32},{32,40},{40,48},{48,56},{56,6... | collective-permute-start | bytes 1572872 | tf_op jit(solution)/shard_map/while/body/eval_jaxpr/ppermute | solution.py:16
  502.1 16.2 %collective-permute-start.2 = (f32[256,4,128]{0,2,1:T(8,128)}, f32[256,4,128]{0,2,1:T(8,128)S(1)}, u32[]{:S(2)}, u32[]{:S(2)}) collective-permute-start(f32[256,4,128]{0,2,1:T(8,128)} %fusion.28), channel_id=1, source_target_pairs={{120,0},{0,8},{8,16},{16,24},{24,32},{32,40},{40,48},{48,56},{56,6... | collective-permute-start | bytes 1572872 | tf_op jit(solution)/shard_map/ppermute | solution.py:16
  502.4 14.9 %collective-permute-start.3 = (bf16[256,4,128]{2,0,1:T(8,128)(2,1)S(1)}, bf16[256,4,128]{2,0,1:T(8,128)(2,1)S(1)}, u32[]{:S(2)}, u32[]{:S(2)}) collective-permute-start(bf16[256,4,128]{2,0,1:T(8,128)(2,1)S(1)} %fusion.29), channel_id=1, source_target_pairs={{120,0},{0,8},{8,16},{16,24},{24,32},{32,40},{40,48},{48,56},{56,6... | collective-permute-start | bytes 786440 | tf_op jit(solution)/shard_map/ppermute | solution.py:16
Sparse Core Ops, SparseCore 0:
  10.8 59.0 all-gather.2
  72.8 54.3 all-gather.4
where the time goes:
time: 528 us; the launch traced here: 526 us
  waiting for transfers between devices  375 us (71%)
  matrix products  65.5 us (12%)
  local copies, waits for them, and re-layouts  57.4 us (11%)
  between operations  14.2 us (3%)
  other arithmetic  11.1 us (2%)
    ppermute x32, waiting for transfers between devices, passed_along(): return lax.ppermute(block, axis, route)  263 us
    all_gather x1, waiting for transfers between devices, local(): lax.all_gather(value_rows, 'seq', axis=0, tiled=True)  57.2 us
    all_gather x1, waiting for transfers between devices, local(): lax.all_gather(key_rows, 'seq', axis=0, tiled=True)  55.4 us
    dot_general x16, matrix products, grads_of(): jnp.einsum('hqk,qhd->khd', score_low, query_heads, preferred_element_type...  18.1 us
    dot_general x16, matrix products, grads_of(): jnp.einsum('hqk,qhd->khd', prob_low, grad_heads, preferred_element_type=j...  17.6 us
    dynamic_slice x16, local copies, waits for them, and re-layouts, stats_turn(): value_piece = lax.dynamic_slice_in_dim(value_all, first_row, row_count, 0)  17.2 us
    dynamic_slice x16, local copies, waits for them, and re-layouts, pick(): lax.dynamic_slice(value_all, (first_row, first_col), (row_count, col_width))  15.6 us
    dynamic_slice x16, local copies, waits for them, and re-layouts, pick(): lax.dynamic_slice(key_all, (first_row, first_col), (row_count, col_width))  15.6 us
  transfers between devices with their start and end apart: 34, of which 33 were waited for; matrix products, arithmetic and copies ran while one was open for 6% of the time, Pallas kernels for 0%

commit v1 on v0

v1 whole, which is shorter than its diff:
```python
import functools

import jax
import jax.numpy as jnp
from jax import lax
from jax.experimental import pallas as pl
from jax.experimental.pallas import tpu as pltpu
from jax.sharding import PartitionSpec as P

HD = 128
BLK = 128
ROWS = 256
MESH = pl.DeviceIdType.MESH
SCALE = HD**-0.5
LOG2E = 1.4426950408889634
BF16 = jnp.bfloat16
F32 = jnp.float32


def place():
    s = lax.axis_index("seq")
    return lax.div(s, 8), lax.rem(lax.div(s, 2), 4), lax.rem(s, 2)


def seq_id(x, y, c):
    return {"seq": x * 8 + y * 2 + c}


def meet(peers):
    barrier = pltpu.get_barrier_semaphore()
    for peer in peers:
        pl.semaphore_signal(barrier, inc=1, device_id=peer, device_id_type=MESH)
    pl.semaphore_wait(barrier, len(peers))


def gather_kernel(q, k, v, g, qg, kv, y_send, y_recv, x_send, x_recv, c_send, c_recv, own):
    x, y, c = place()
    x_peer, c_peer = seq_id(1 - x, y, c), seq_id(x, y, 1 - c)
    y_of = lambda d: lax.rem(y + d, 4)
    meet([x_peer, c_peer] + [seq_id(x, y_of(d), c) for d in (1, 2, 3)])

    def chunk(xx, yy, cc):
        return xx * 8 + yy * 2 + cc

    def cols(ref, head):
        return ref.at[:, pl.ds(pl.multiple_of(head * HD, HD), HD)]

    def remote(src, dst, send, recv, device):
        return pltpu.make_async_remote_copy(
            src_ref=src, dst_ref=dst, send_sem=send, recv_sem=recv, device_id=device, device_id_type=MESH
        )

    sends = []

    def go(copy):
        copy.start()
        sends.append(copy)

    here = chunk(x, y, c)
    own_copies = [
        pltpu.make_async_copy(cols(k, y), kv.at[here, 0], own.at[0]),
        pltpu.make_async_copy(cols(v, y), kv.at[here, 1], own.at[1]),
        pltpu.make_async_copy(cols(q, y), qg.at[y, 0], own.at[2]),
        pltpu.make_async_copy(cols(g, y), qg.at[y, 1], own.at[3]),
    ]
    for copy in own_copies:
        copy.start()
    for a, ref in enumerate((k, v)):
        for d in (1, 3, 2):
            go(remote(cols(ref, y_of(d)), kv.at[here, a], y_send.at[a, d], y_recv.at[a, d], seq_id(x, y_of(d), c)))
    for copy in own_copies[:2]:
        copy.wait()

    def onward(d):
        there = chunk(x, y_of(d), c)
        go(remote(kv.at[there], kv.at[there], x_send.at[d], x_recv.at[d], x_peer))
        go(remote(kv.at[there], kv.at[there], c_send.at[0, d], c_recv.at[0, d], c_peer))

    onward(0)
    for a, ref in enumerate((q, g)):
        for d in (1, 3, 2):
            go(remote(cols(ref, y_of(d)), qg.at[y, a], y_send.at[a + 2, d], y_recv.at[a + 2, d], seq_id(x, y_of(d), c)))

    def arrived(dst, recv):
        remote(dst, dst, own.at[0], recv, x_peer).wait_recv()

    for d in (3, 1, 2):
        there = chunk(x, y_of(d), c)
        for a in range(2):
            arrived(kv.at[there, a], y_recv.at[a, 4 - d])
        onward(d)
    for d in (0, 3, 1, 2):
        there = chunk(1 - x, y_of(d), c)
        arrived(kv.at[there], x_recv.at[d])
        go(remote(kv.at[there], kv.at[there], c_send.at[1, d], c_recv.at[1, d], c_peer))
    for d in (3, 1, 2):
        for a in range(2):
            arrived(qg.at[y_of(d), a], y_recv.at[a + 2, 4 - d])
    for d in range(4):
        arrived(kv.at[chunk(x, y_of(d), 1 - c)], c_recv.at[0, d])
        arrived(kv.at[chunk(1 - x, y_of(d), 1 - c)], c_recv.at[1, d])
    for copy in own_copies[2:]:
        copy.wait()
    for copy in sends:
        copy.wait_send()


def gather(q, k, v, g):
    dma = pltpu.SemaphoreType.DMA
    return pl.pallas_call(
        gather_kernel,
        out_shape=(
            jax.ShapeDtypeStruct((4, 2, ROWS, HD), BF16),
            jax.ShapeDtypeStruct((16, 2, ROWS, HD), BF16),
        ),
        in_specs=[pl.BlockSpec(memory_space=pl.ANY)] * 4,
        out_specs=(pl.BlockSpec(memory_space=pl.ANY),) * 2,
        scratch_shapes=[
            dma((4, 4)), dma((4, 4)), dma((4,)), dma((4,)), dma((2, 4)), dma((2, 4)), dma((4,)),
        ],
        compiler_params=pltpu.CompilerParams(collective_id=0, has_side_effects=True),
        name="exchange_in",
    )(q, k, v, g)


def grads_kernel(blocks, qg, kv, dq_out, dkv_out, s_buf, d_buf, dkv_acc):
    x, y, c = place()
    end0 = blocks[0]
    end1 = end0 + blocks[1]

    def seg(b):
        return (b >= end0).astype(jnp.int32) + (b >= end1).astype(jnp.int32)

    dkv_acc[...] = jnp.zeros_like(dkv_acc)
    lane = lax.broadcasted_iota(jnp.int32, (1, ROWS), 1)
    nt = (((1,), (1,)), ((), ()))
    tn = (((0,), (0,)), ((), ()))

    def of_chunk(i, carry):
        b0 = 16 * x + 4 * i + 2 * c
        seg0, seg1 = seg(b0), seg(b0 + 1)
        start = jnp.where(seg0 == 0, 0, jnp.where(seg0 == 1, end0, end1))
        stop = jnp.where(seg1 == 0, end0, jnp.where(seg1 == 1, end1, 32))
        lo, hi = lax.div(start, 2), lax.div(stop + 1, 2)
        lane_seg = jnp.where(lane < BLK, seg0, seg1)
        q_i, g_i = qg[i, 0], qg[i, 1]

        def scores(j, m):
            s_t = lax.dot_general(kv[j, 0], q_i, nt, preferred_element_type=F32)
            s_buf[j] = s_t
            for half in range(2):
                top = jnp.max(s_t[half * BLK : (half + 1) * BLK], axis=0, keepdims=True)
                m = jnp.maximum(m, jnp.where(lane_seg == seg(2 * j + half), top, -1e30))
            return m

        m = lax.fori_loop(lo, hi, scores, jnp.full((1, ROWS), -1e30, F32))
        m = m * (SCALE * LOG2E)

        def sums(j, carried):
            l, r = carried
            d_t = lax.dot_general(kv[j, 1], g_i, nt, preferred_element_type=F32)
            d_buf[j] = d_t
            for half in range(2):
                rows = slice(half * BLK, (half + 1) * BLK)
                top = jnp.where(lane_seg == seg(2 * j + half), m, 1e30)
                e = jnp.exp2(s_buf[j, rows] * (SCALE * LOG2E) - top)
                s_buf[j, rows] = e
                l = l + jnp.sum(e, axis=0, keepdims=True)
                r = r + jnp.sum(e * d_t[rows], axis=0, keepdims=True)
            return l, r

        zero = jnp.zeros((1, ROWS), F32)
        l, r = lax.fori_loop(lo, hi, sums, (zero, zero))
        inv = 1.0 / l
        delta = r * inv

        def products(j, dq):
            p = s_buf[j] * inv
            ds = (p * (d_buf[j] - delta)).astype(BF16)
            dkv_acc[j, 1] += jnp.dot(p.astype(BF16), g_i, preferred_element_type=F32)
            dkv_acc[j, 0] += jnp.dot(ds, q_i, preferred_element_type=F32)
            return dq + lax.dot_general(ds, kv[j, 0], tn, preferred_element_type=F32)

        dq = lax.fori_loop(lo, hi, products, jnp.zeros((ROWS, HD), F32))
        dq_out[i] = (dq * SCALE).astype(BF16)
        return carry

    lax.fori_loop(0, 4, of_chunk, 0)
    dkv_out[:, 0] = (dkv_acc[:, 0] * SCALE).astype(BF16)
    dkv_out[:, 1] = dkv_acc[:, 1].astype(BF16)


def grads(sample_blocks, qg, kv):
    return pl.pallas_call(
        grads_kernel,
        out_shape=(
            jax.ShapeDtypeStruct((4, ROWS, HD), BF16),
            jax.ShapeDtypeStruct((16, 2, ROWS, HD), BF16),
        ),
        in_specs=[pl.BlockSpec(memory_space=pltpu.SMEM)] + [pl.BlockSpec(memory_space=pltpu.VMEM)] * 2,
        out_specs=(pl.BlockSpec(memory_space=pltpu.VMEM),) * 2,
        scratch_shapes=[
            pltpu.VMEM((16, ROWS, ROWS), F32),
            pltpu.VMEM((16, ROWS, ROWS), F32),
            pltpu.VMEM((16, 2, ROWS, HD), F32),
        ],
        compiler_params=pltpu.CompilerParams(vmem_limit_bytes=48 << 20),
        name="grads",
    )(sample_blocks, qg, kv)


def scatter_kernel(dq, dkv, dq_out, dk_out, dv_out, got_c, got_x, half_out, final, part,
                   c_send, c_recv, x_send, x_recv, y_send, y_recv, own):
    x, y, c = place()
    x_peer, c_peer = seq_id(1 - x, y, c), seq_id(x, y, 1 - c)
    y_of = lambda d: lax.rem(y + d, 4)
    meet([x_peer, c_peer] + [seq_id(x, y_of(d), c) for d in (1, 2, 3)])

    def chunk(xx, yy, cc):
        return xx * 8 + yy * 2 + cc

    def cols(ref, head):
        return ref.at[:, pl.ds(pl.multiple_of(head * HD, HD), HD)]

    def remote(src, dst, send, recv, device):
        return pltpu.make_async_remote_copy(
            src_ref=src, dst_ref=dst, send_sem=send, recv_sem=recv, device_id=device, device_id_type=MESH
        )

    sends = []

    def go(copy):
        copy.start()
        sends.append(copy)

    def arrived(dst, recv):
        remote(dst, dst, own.at[0], recv, x_peer).wait_recv()

    outs = (dq_out, dk_out, dv_out)
    order = (3, 1, 2, 0)
    for far in (1, 0):
        for d in order:
            xx = 1 - x if far else x
            go(remote(dkv.at[chunk(xx, y_of(d), 1 - c)], got_c.at[far, y_of(d)], c_send.at[far, d], c_recv.at[far, d], c_peer))
    for d in (1, 3, 2):
        go(remote(dq.at[y_of(d)], cols(dq_out, y), y_send.at[0, d], y_recv.at[0, d], seq_id(x, y_of(d), c)))
    own_q = pltpu.make_async_copy(dq.at[y], cols(dq_out, y), own.at[1])
    own_q.start()
    for d in order:
        yy = y_of(d)
        arrived(got_c.at[1, yy], c_recv.at[1, d])
        mine = dkv[chunk(1 - x, yy, c)].astype(F32) + got_c[1, yy].astype(F32)
        half_out[yy] = mine.astype(BF16)
        go(remote(half_out.at[yy], got_x.at[yy], x_send.at[d], x_recv.at[d], x_peer))
    for d in order:
        yy = y_of(d)
        arrived(got_c.at[0, yy], c_recv.at[0, d])
        part[yy] = dkv[chunk(x, yy, c)].astype(F32) + got_c[0, yy].astype(F32)
    own_kv = []
    for d in order:
        yy = y_of(d)
        arrived(got_x.at[yy], x_recv.at[d])
        final[yy] = (part[yy] + got_x[yy].astype(F32)).astype(BF16)
        for a in range(2):
            if d:
                go(remote(final.at[yy, a], cols(outs[a + 1], y), y_send.at[a + 1, d], y_recv.at[a + 1, d], seq_id(x, yy, c)))
            else:
                copy = pltpu.make_async_copy(final.at[yy, a], cols(outs[a + 1], y), own.at[2 + a])
                copy.start()
                own_kv.append(copy)
    for d in (3, 1, 2):
        for a in range(3):
            arrived(cols(outs[a], y_of(d)), y_recv.at[a, 4 - d])
    own_q.wait()
    for copy in own_kv:
        copy.wait()
    for copy in sends:
        copy.wait_send()


def scatter(dq, dkv):
    dma = pltpu.SemaphoreType.DMA
    out = jax.ShapeDtypeStruct((ROWS, 4 * HD), BF16)
    return pl.pallas_call(
        scatter_kernel,
        out_shape=(out,) * 3,
        in_specs=[pl.BlockSpec(memory_space=pltpu.VMEM)] * 2,
        out_specs=(pl.BlockSpec(memory_space=pltpu.VMEM),) * 3,
        scratch_shapes=[
            pltpu.VMEM((2, 4, 2, ROWS, HD), BF16),
            pltpu.VMEM((4, 2, ROWS, HD), BF16),
            pltpu.VMEM((4, 2, ROWS, HD), BF16),
            pltpu.VMEM((4, 2, ROWS, HD), BF16),
            pltpu.VMEM((4, 2, ROWS, HD), F32),
            dma((2, 4)), dma((2, 4)), dma((4,)), dma((4,)), dma((3, 4)), dma((3, 4)), dma((4,)),
        ],
        compiler_params=pltpu.CompilerParams(
            collective_id=1, has_side_effects=True, vmem_limit_bytes=32 << 20
        ),
        name="exchange_out",
    )(dq, dkv)


def local(query, key_rows, value_rows, out_grad, sample_blocks):
    qg, kv = gather(query, key_rows, value_rows, out_grad)
    dq, dkv = grads(sample_blocks, qg, kv)
    return scatter(dq, dkv)


def solution(mesh):
    spec = P("seq", "head")
    return jax.shard_map(
        local, mesh=mesh, in_specs=(spec, spec, spec, spec, P()), out_specs=(spec,) * 3, check_vma=False
    )
```

time: 528 us -> 79 us (0.15)
  waiting for transfers between devices: 375 us -> 0 us
  Pallas kernels: 0 us -> 72.8 us
  matrix products: 65.5 us -> 0 us
  local copies, waits for them, and re-layouts: 57.4 us -> 5.39 us
  between operations: 14.2 us -> 0.67 us
  other arithmetic: 11.1 us -> 0 us
    ppermute x32 -> x0, waiting for transfers between devices: 263 us -> none  [passed_along(): return lax.ppermute(block, axis, route)]
    all_gather x2 -> x0, waiting for transfers between devices: 113 us -> none  [the longest x1 57.2 us: local(): lax.all_gather(value_rows, 'seq', axis=0, tiled=True)]
    pallas_call x0 -> x3, Pallas kernels: none -> 72.8 us  [the longest x1 25.3 us: scatter(): pl.pallas_call(scatter_kernel, out_shape=(out,) * 3, in_specs=[pl.BlockSp...]
    dot_general x112 -> x0, matrix products: 65.5 us -> none  [the longest x16 18.1 us: grads_of(): jnp.einsum('hqk,qhd->khd', score_low, query_heads, preferred_element_type...]
    dynamic_slice x48 -> x0, local copies, waits for them, and re-layouts: 48.3 us -> none  [the longest x16 17.2 us: stats_turn(): value_piece = lax.dynamic_slice_in_dim(value_all, first_row, row_count, 0)]
    reduce_sum x48 -> x0, other arithmetic: 6.06 us -> none  [the longest x16 3.33 us: stats_step(): jnp.sum(exp_terms, axis=2)]
  transfers between devices with their start and end apart: 34 -> 0, of which waited for: 33 -> 0; matrix products, arithmetic and copies ran while one was open for 6% -> 0% of each run, Pallas kernels for 0% -> 0%
where the time goes in v1:
time: 79 us; the launch traced here: 78.8 us
  Pallas kernels  72.8 us (92%)
  local copies, waits for them, and re-layouts  5.39 us (7%)
    pallas_call x1, Pallas kernels, scatter(): pl.pallas_call(scatter_kernel, out_shape=(out,) * 3, in_specs=[pl.BlockSp...  25.3 us
    pallas_call x1, Pallas kernels, gather(): pl.pallas_call(gather_kernel, out_shape=(jax.ShapeDtypeStruct((4, 2, ROWS...  25.3 us
    pallas_call x1, Pallas kernels, grads(): pl.pallas_call(grads_kernel, out_shape=(jax.ShapeDtypeStruct((4, ROWS, HD...  22.1 us
    unnamed x9, local copies, waits for them, and re-layouts  5.39 us

profile of v1, /device:TPU:0, one launch (start us, length us, event | category | flops | bytes accessed | tf_op | source)
XLA Modules:
  0.0 78.8 jit_solution(9602328687213670950)
XLA Ops:
  0.6 25.3 %exchange_in.1 = (bf16[4,2,256,128]{3,2,1,0:T(8,128)(2,1)}, bf16[16,2,256,128]{3,2,1,0:T(8,128)(2,1)}) custom-call(bf16[256,512]{1,0:T(8,128)(2,1)} %q.1, bf16[256,512]{1,0:T(8,128)(2,1)} %k.1, bf16[256,512]{1,0:T(8,128)(2,1)} %v.1, bf16[256,512]{1,0:T(8,128)(2,1)} %g.1), custom_call_target="tpu_custom_call" | custom-call | tf_op jit(solution)/shard_map/exchange_in/pallas_call | solution.py:110
  26.0 0.0 copy-start
  26.0 1.6 %copy-done = bf16[16,2,256,128]{3,2,1,0:T(8,128)(2,1)S(1)} copy-done((bf16[16,2,256,128]{3,2,1,0:T(8,128)(2,1)S(1)}, bf16[16,2,256,128]{3,2,1,0:T(8,128)(2,1)}, u32[]{:S(2)}) %copy-start) | copy-done | bytes 2097176
  27.5 0.0 copy-start.1
  27.5 1.0 %copy-done.1 = bf16[4,2,256,128]{3,2,1,0:T(8,128)(2,1)S(1)} copy-done((bf16[4,2,256,128]{3,2,1,0:T(8,128)(2,1)S(1)}, bf16[4,2,256,128]{3,2,1,0:T(8,128)(2,1)}, u32[]{:S(2)}) %copy-start.1) | copy-done | bytes 524312
  28.6 0.0 copy-start.2
  28.6 0.7 copy-done.2
  29.2 22.1 %grads.1 = (bf16[4,256,128]{2,1,0:T(8,128)(2,1)S(1)}, bf16[16,2,256,128]{3,2,1,0:T(8,128)(2,1)S(1)}) custom-call(s32[3]{0:T(128)S(1)} %copy-done.2, bf16[4,2,256,128]{3,2,1,0:T(8,128)(2,1)S(1)} %copy-done.1, bf16[16,2,256,128]{3,2,1,0:T(8,128)(2,1)S(1)} %copy-done), custom_call_target="tpu_custom_call" | custom-call | tf_op jit(solution)/shard_map/grads/pallas_call | solution.py:194
  51.4 25.3 %exchange_out.1 = (bf16[256,512]{1,0:T(8,128)(2,1)S(1)}, bf16[256,512]{1,0:T(8,128)(2,1)S(1)}, bf16[256,512]{1,0:T(8,128)(2,1)S(1)}) custom-call(bf16[4,256,128]{2,1,0:T(8,128)(2,1)S(1)} %get-tuple-element.9.dq, bf16[16,2,256,128]{3,2,1,0:T(8,128)(2,1)S(1)} %get-tuple-element.10.dkv), custom_call_target="tpu_custom_call" | custom-call | tf_op jit(solution)/shard_map/exchange_out/pallas_call | solution.py:284
  76.7 0.7 copy.11
  77.4 0.7 copy.12
  78.1 0.7 copy.13
Async XLA Ops:
  26.0 1.6 %copy-start = (bf16[16,2,256,128]{3,2,1,0:T(8,128)(2,1)S(1)}, bf16[16,2,256,128]{3,2,1,0:T(8,128)(2,1)}, u32[]{:S(2)}) copy-start(bf16[16,2,256,128]{3,2,1,0:T(8,128)(2,1)} %get-tuple-element.8.kv) | copy-start | bytes 6291460
  27.5 1.0 %copy-start.1 = (bf16[4,2,256,128]{3,2,1,0:T(8,128)(2,1)S(1)}, bf16[4,2,256,128]{3,2,1,0:T(8,128)(2,1)}, u32[]{:S(2)}) copy-start(bf16[4,2,256,128]{3,2,1,0:T(8,128)(2,1)} %get-tuple-element.7.qg) | copy-start | bytes 1572868
  28.6 0.7 copy-start.2

commit v2 on v0

v2 whole, which is shorter than its diff:
```python
import jax
import jax.numpy as jnp
from jax import lax
from jax.experimental import pallas as pl
from jax.experimental.pallas import tpu as pltpu
from jax.sharding import PartitionSpec as P

HD = 128
BLK = 128
ROWS = 256
QUERIES = 1024
MESH = pl.DeviceIdType.MESH
SCALE = HD**-0.5
EXP2_SCALE = SCALE * 1.4426950408889634
MASKED = -1e30
BF16 = jnp.bfloat16
F32 = jnp.float32
NT = (((1,), (1,)), ((), ()))


def place():
    s = lax.axis_index("seq")
    return lax.div(s, 8), lax.rem(lax.div(s, 2), 4), lax.rem(s, 2)


def seq_id(x, y, c):
    return {"seq": x * 8 + y * 2 + c}


def chunk(x, y, c):
    return x * 8 + y * 2 + c


def cols(ref, head):
    return ref.at[:, pl.ds(pl.multiple_of(head * HD, HD), HD)]


def rows(i):
    return pl.ds(pl.multiple_of(i * ROWS, ROWS), ROWS)


def kernel(
    blocks, q, k, v, g, dq_out, dk_out, dv_out,
    kv, qg, e_buf, d_buf, m_hist, stats, dq_acc, dq_low,
    to_core, got_core, keep, to_x, got_x, final, ends,
    y_send, y_recv, x_send, x_recv, c_send, c_recv, own,
    c2_send, c2_recv, x2_send, x2_recv, y2_send, y2_recv,
):
    x, y, c = place()
    x_peer, c_peer = seq_id(1 - x, y, c), seq_id(x, y, 1 - c)
    outs = (dq_out, dk_out, dv_out)

    def y_of(d):
        return lax.rem(y + d, 4)

    def remote(src, dst, send, recv, device):
        return pltpu.make_async_remote_copy(
            src_ref=src, dst_ref=dst, send_sem=send, recv_sem=recv, device_id=device, device_id_type=MESH
        )

    def arrived(dst, recv):
        remote(dst, dst, own.at[0], recv, x_peer).wait_recv()

    def sent(src, send):
        remote(src, src, send, own.at[0], x_peer).wait_send()

    here = chunk(x, y, c)
    own_copies = [
        pltpu.make_async_copy(cols(k, y), kv.at[here, 0], own.at[1]),
        pltpu.make_async_copy(cols(v, y), kv.at[here, 1], own.at[2]),
        pltpu.make_async_copy(cols(q, y), qg.at[0, rows(y)], own.at[3]),
        pltpu.make_async_copy(cols(g, y), qg.at[1, rows(y)], own.at[4]),
        pltpu.make_async_copy(blocks, ends, own.at[5]),
    ]
    for copy in own_copies:
        copy.start()

    peers = [x_peer, c_peer] + [seq_id(x, y_of(d), c) for d in (1, 2, 3)]
    barrier = pltpu.get_barrier_semaphore()
    for peer in peers:
        pl.semaphore_signal(barrier, inc=1, device_id=peer, device_id_type=MESH)
    pl.semaphore_wait(barrier, len(peers))

    sends = []

    def go(copy):
        copy.start()
        sends.append(copy)

    def y_keys(d):
        for a, ref in enumerate((k, v)):
            go(remote(cols(ref, y_of(d)), kv.at[here, a], y_send.at[a, d], y_recv.at[a, d], seq_id(x, y_of(d), c)))

    def y_queries(d):
        for a, ref in enumerate((q, g)):
            go(remote(cols(ref, y_of(d)), qg.at[a, rows(y)], y_send.at[a + 2, d], y_recv.at[a + 2, d], seq_id(x, y_of(d), c)))

    def onward(d):
        there = kv.at[chunk(x, y_of(d), c)]
        go(remote(there, there, x_send.at[d], x_recv.at[d], x_peer))
        go(remote(there, there, c_send.at[0, d], c_recv.at[0, d], c_peer))

    y_keys(1)
    y_keys(3)
    for copy in own_copies[:2]:
        copy.wait()
    onward(0)
    y_queries(1)
    y_queries(3)
    y_keys(2)
    y_queries(2)
    for d in (3, 1, 2):
        for a in range(2):
            arrived(kv.at[chunk(x, y_of(d), c), a], y_recv.at[a, 4 - d])
        onward(d)
    for copy in own_copies[2:]:
        copy.wait()
    for d in (3, 1, 2):
        for a in range(2):
            arrived(qg.at[a, rows(y_of(d))], y_recv.at[a + 2, 4 - d])
    for d in range(4):
        arrived(kv.at[chunk(x, y_of(d), 1 - c)], c_recv.at[0, d])

    end0 = ends[0]
    end1 = end0 + ends[1]
    lane = lax.broadcasted_iota(jnp.int32, (1, QUERIES), 1)
    lane_block = 16 * x + 2 * c + 4 * (lane >> 8) + ((lane >> 7) & 1)
    lane_seg = (lane_block >= end0).astype(jnp.int32) + (lane_block >= end1).astype(jnp.int32)
    stats[0] = jnp.full((1, QUERIES), MASKED, F32)
    stats[1] = jnp.zeros((1, QUERIES), F32)
    stats[2] = jnp.zeros((1, QUERIES), F32)

    def pass_a(t):
        for i in range(4):
            sl = slice(i * ROWS, (i + 1) * ROWS)
            s = lax.dot_general(kv[t, 0], qg[0, sl], NT, preferred_element_type=F32)
            d = lax.dot_general(kv[t, 1], qg[1, sl], NT, preferred_element_type=F32)
            m, l, r = stats[0, :, sl], stats[1, :, sl], stats[2, :, sl]
            halves = (slice(0, BLK), slice(BLK, ROWS))
            allowed = []
            new = m
            for h, half in enumerate(halves):
                key_block = 2 * t + h
                key_seg = (key_block >= end0).astype(jnp.int32) + (key_block >= end1).astype(jnp.int32)
                allowed.append(lane_seg[:, sl] == key_seg)
                top = jnp.max(s[half], axis=0, keepdims=True) * EXP2_SCALE
                new = jnp.maximum(new, jnp.where(allowed[h], top, MASKED))
            factor = jnp.exp2(m - new)
            l, r = l * factor, r * factor
            for h, half in enumerate(halves):
                top = jnp.where(allowed[h], new, -MASKED)
                e = jnp.exp2(s[half] * EXP2_SCALE - top)
                l = l + jnp.sum(e, axis=0, keepdims=True)
                r = r + jnp.sum(e * d[half], axis=0, keepdims=True)
                e_buf[t, half, sl] = e
            d_buf[t, :, sl] = d
            stats[0, :, sl], stats[1, :, sl], stats[2, :, sl] = new, l, r
            m_hist[t, :, sl] = new

    def a_near(n, carry):
        d = n + n // 2 - 2 * (n // 3)
        pass_a(chunk(x, y_of(d), c))
        far = kv.at[chunk(1 - x, y_of(d), c)]
        arrived(far, x_recv.at[d])
        remote(far, far, c_send.at[1, d], c_recv.at[1, d], c_peer).start()
        pass_a(chunk(x, y_of(d), 1 - c))
        return carry

    def a_far(n, carry):
        d = n + n // 2 - 2 * (n // 3)
        pass_a(chunk(1 - x, y_of(d), c))
        arrived(kv.at[chunk(1 - x, y_of(d), 1 - c)], c_recv.at[1, d])
        pass_a(chunk(1 - x, y_of(d), 1 - c))
        return carry

    lax.fori_loop(0, 4, a_near, 0)
    lax.fori_loop(0, 4, a_far, 0)

    inv = 1.0 / stats[1]
    stats[2] = stats[2] * inv
    stats[1] = inv
    dq_acc[...] = jnp.zeros_like(dq_acc)

    def pass_b(t, out):
        factor = jnp.exp2(m_hist[t] - stats[0]) * stats[1]
        p = e_buf[t] * factor
        ds = (p * (d_buf[t] - stats[2])).astype(BF16)
        out[1] = jnp.dot(p.astype(BF16), qg[1], preferred_element_type=F32)
        out[0] = jnp.dot(ds, qg[0], preferred_element_type=F32)
        dq_acc[...] += jnp.dot(kv[t, 0].T, ds, preferred_element_type=F32)

    def core_copy(far, d):
        return remote(to_core.at[far, d], got_core.at[far, d], c2_send.at[far, d], c2_recv.at[far, d], c_peer)

    def x_copy(d):
        return remote(to_x.at[d], got_x.at[d], x2_send.at[d], x2_recv.at[d], x_peer)

    def y_copy(a, d, src):
        return remote(src, cols(outs[a], y), y2_send.at[a, d], y2_recv.at[a, d], seq_id(x, y_of(d), c))

    def finish_far(d):
        arrived(got_core.at[0, d], c2_recv.at[0, d])
        to_x[d] = (keep[0, d] + got_core[0, d]).astype(BF16)
        x_copy(d).start()

    def sum_near(d):
        arrived(got_core.at[1, d], c2_recv.at[1, d])
        keep[1, d] = keep[1, d] + got_core[1, d]

    def finish_near(d):
        arrived(got_x.at[d], x2_recv.at[d])
        total = keep[1, d] + got_x[d].astype(F32)
        final[d, 0] = (total[0] * SCALE).astype(BF16)
        final[d, 1] = total[1].astype(BF16)

    def b_far(n, carry):
        d = lax.rem(n + 1, 4)
        pass_b(chunk(1 - x, y_of(d), 1 - c), to_core.at[0, d])
        core_copy(0, d).start()

        @pl.when(n > 0)
        def _():
            finish_far(n)

        pass_b(chunk(1 - x, y_of(d), c), keep.at[0, d])
        return carry

    def b_near(n, carry):
        d = lax.rem(n + 1, 4)
        pass_b(chunk(x, y_of(d), 1 - c), to_core.at[1, d])
        core_copy(1, d).start()

        @pl.when(n == 0)
        def _():
            finish_far(0)

        @pl.when(n > 0)
        def _():
            sum_near(n)

        @pl.when(n > 1)
        def _():
            finish_near(n - 1)
            for a in range(2):
                y_copy(a + 1, n - 1, final.at[n - 1, a]).start()

        pass_b(chunk(x, y_of(d), c), keep.at[1, d])
        return carry

    lax.fori_loop(0, 4, b_far, 0)
    lax.fori_loop(0, 4, b_near, 0)

    for i in range(4):
        dq_low[i * ROWS : (i + 1) * ROWS] = (dq_acc[:, i * ROWS : (i + 1) * ROWS].T * SCALE).astype(BF16)
    for d in (2, 1, 3):
        y_copy(0, d, dq_low.at[rows(y_of(d))]).start()
    last = [pltpu.make_async_copy(dq_low.at[rows(y)], cols(dq_out, y), own.at[1])]
    last[0].start()
    sum_near(0)
    finish_near(3)
    for a in range(2):
        y_copy(a + 1, 3, final.at[3, a]).start()
    finish_near(0)
    for a in range(2):
        copy = pltpu.make_async_copy(final.at[0, a], cols(outs[a + 1], y), own.at[2 + a])
        copy.start()
        last.append(copy)

    for d in (3, 2, 1):
        for a in range(3):
            arrived(cols(outs[a], y_of(d)), y2_recv.at[a, 4 - d])
    for copy in last:
        copy.wait()
    for copy in sends:
        copy.wait_send()
    for d in range(4):
        sent(kv.at[0], c_send.at[1, d])
        sent(to_core.at[0, d], c2_send.at[0, d])
        sent(to_core.at[1, d], c2_send.at[1, d])
        sent(to_x.at[d], x2_send.at[d])
    for d in (1, 2, 3):
        for a in range(3):
            sent(cols(outs[a], y), y2_send.at[a, d])


def local(query, key_rows, value_rows, out_grad, sample_blocks):
    dma = pltpu.SemaphoreType.DMA
    vmem = pltpu.VMEM
    out = jax.ShapeDtypeStruct((ROWS, 4 * HD), BF16)
    return pl.pallas_call(
        kernel,
        out_shape=(out,) * 3,
        in_specs=[pl.BlockSpec(memory_space=pl.ANY)] * 5,
        out_specs=(pl.BlockSpec(memory_space=vmem),) * 3,
        scratch_shapes=[
            vmem((16, 2, ROWS, HD), BF16),
            vmem((2, QUERIES, HD), BF16),
            vmem((16, ROWS, QUERIES), F32),
            vmem((16, ROWS, QUERIES), F32),
            vmem((16, 1, QUERIES), F32),
            vmem((3, 1, QUERIES), F32),
            vmem((HD, QUERIES), F32),
            vmem((QUERIES, HD), BF16),
            vmem((2, 4, 2, ROWS, HD), F32),
            vmem((2, 4, 2, ROWS, HD), F32),
            vmem((2, 4, 2, ROWS, HD), F32),
            vmem((4, 2, ROWS, HD), BF16),
            vmem((4, 2, ROWS, HD), BF16),
            vmem((4, 2, ROWS, HD), BF16),
            pltpu.SMEM((3,), jnp.int32),
            dma((4, 4)), dma((4, 4)), dma((4,)), dma((4,)), dma((2, 4)), dma((2, 4)), dma((6,)),
            dma((2, 4)), dma((2, 4)), dma((4,)), dma((4,)), dma((3, 4)), dma((3, 4)),
        ],
        compiler_params=pltpu.CompilerParams(
            collective_id=0, has_side_effects=True, vmem_limit_bytes=60 << 20
        ),
        name="attention_grads",
    )(sample_blocks, query, key_rows, value_rows, out_grad)


def solution(mesh):
    spec = P("seq", "head")
    return jax.shard_map(
        local, mesh=mesh, in_specs=(spec, spec, spec, spec, P()), out_specs=(spec,) * 3, check_vma=False
    )
```

time: 528 us -> 54.6 us (0.10)
  waiting for transfers between devices: 375 us -> 0 us
  matrix products: 65.5 us -> 0 us
  local copies, waits for them, and re-layouts: 57.4 us -> 3.46 us
  Pallas kernels: 0 us -> 49.6 us
  between operations: 14.2 us -> 0.65 us
  other arithmetic: 11.1 us -> 0 us
    ppermute x32 -> x0, waiting for transfers between devices: 263 us -> none  [passed_along(): return lax.ppermute(block, axis, route)]
    all_gather x2 -> x0, waiting for transfers between devices: 113 us -> none  [the longest x1 57.2 us: local(): lax.all_gather(value_rows, 'seq', axis=0, tiled=True)]
    dot_general x112 -> x0, matrix products: 65.5 us -> none  [the longest x16 18.1 us: grads_of(): jnp.einsum('hqk,qhd->khd', score_low, query_heads, preferred_element_type...]
    pallas_call x0 -> x1, Pallas kernels: none -> 49.6 us  [local(): pl.pallas_call(kernel, out_shape=(out,) * 3, in_specs=[pl.BlockSpec(memor...]
    dynamic_slice x48 -> x0, local copies, waits for them, and re-layouts: 48.3 us -> none  [the longest x16 17.2 us: stats_turn(): value_piece = lax.dynamic_slice_in_dim(value_all, first_row, row_count, 0)]
    reduce_sum x48 -> x0, other arithmetic: 6.06 us -> none  [the longest x16 3.33 us: stats_step(): jnp.sum(exp_terms, axis=2)]
  transfers between devices with their start and end apart: 34 -> 0, of which waited for: 33 -> 0; matrix products, arithmetic and copies ran while one was open for 6% -> 0% of each run, Pallas kernels for 0% -> 0%
where the time goes in v2:
time: 54.6 us; the launch traced here: 53.7 us
  Pallas kernels  49.6 us (91%)
  local copies, waits for them, and re-layouts  3.46 us (6%)
  between operations  0.65 us (1%)
    pallas_call x1, Pallas kernels, local(): pl.pallas_call(kernel, out_shape=(out,) * 3, in_specs=[pl.BlockSpec(memor...  49.6 us
    unnamed x7, local copies, waits for them, and re-layouts  3.46 us

profile of v2, /device:TPU:0, one launch (start us, length us, event | category | flops | bytes accessed | tf_op | source)
XLA Modules:
  0.0 53.7 jit_solution(10117025248326181811)
XLA Ops:
  0.6 49.6 %attention_grads.1 = (bf16[256,512]{1,0:T(8,128)(2,1)}, bf16[256,512]{1,0:T(8,128)(2,1)}, bf16[256,512]{1,0:T(8,128)(2,1)}) custom-call(s32[3]{0:T(128)} %blocks.1, bf16[256,512]{1,0:T(8,128)(2,1)} %q.1, bf16[256,512]{1,0:T(8,128)(2,1)} %k.1, bf16[256,512]{1,0:T(8,128)(2,1)} %v.1, bf16[256,512]{1,0:T(8,128)(2,1)} %g.1), custom_call_target="tpu_custom_call" | custom-call | tf_op jit(solution)/shard_map/attention_grads/pallas_call | solution.py:290
  50.2 0.0 copy-start.1
  50.2 1.7 %copy.11 = bf16[256,512]{1,0:T(8,128)(2,1)} copy(bf16[256,512]{1,0:T(8,128)(2,1)} %get-tuple-element.6) | data formatting | bytes 524288
  51.9 0.0 copy-done.1
  51.9 0.0 copy-start
  51.9 0.7 %copy.12 = bf16[256,512]{1,0:T(8,128)(2,1)} copy(bf16[256,512]{1,0:T(8,128)(2,1)S(1)} %copy-done.1) | data formatting | bytes 524288
  52.6 0.3 copy-done
  53.0 0.7 %copy.13 = bf16[256,512]{1,0:T(8,128)(2,1)} copy(bf16[256,512]{1,0:T(8,128)(2,1)S(1)} %copy-done) | data formatting | bytes 524288
Async XLA Ops:
  50.2 1.7 %copy-start.1 = (bf16[256,512]{1,0:T(8,128)(2,1)S(1)}, bf16[256,512]{1,0:T(8,128)(2,1)}, u32[]{:S(2)}) copy-start(bf16[256,512]{1,0:T(8,128)(2,1)} %get-tuple-element.7) | copy-start | bytes 786436
  51.9 1.0 %copy-start = (bf16[256,512]{1,0:T(8,128)(2,1)S(1)}, bf16[256,512]{1,0:T(8,128)(2,1)}, u32[]{:S(2)}) copy-start(bf16[256,512]{1,0:T(8,128)(2,1)} %get-tuple-element.8) | copy-start | bytes 786436

commit v3 on v2

--- a/solution.py
+++ b/solution.py
@@ -9,6 +9,7 @@
 BLK = 128
 ROWS = 256
 QUERIES = 1024
+SLOT_OF = {0: 0, 1: 1, 3: 2, 2: 3}
 MESH = pl.DeviceIdType.MESH
 SCALE = HD**-0.5
 EXP2_SCALE = SCALE * 1.4426950408889634
@@ -68,8 +69,8 @@
     own_copies = [
         pltpu.make_async_copy(cols(k, y), kv.at[here, 0], own.at[1]),
         pltpu.make_async_copy(cols(v, y), kv.at[here, 1], own.at[2]),
-        pltpu.make_async_copy(cols(q, y), qg.at[0, rows(y)], own.at[3]),
-        pltpu.make_async_copy(cols(g, y), qg.at[1, rows(y)], own.at[4]),
+        pltpu.make_async_copy(cols(q, y), qg.at[0, rows(0)], own.at[3]),
+        pltpu.make_async_copy(cols(g, y), qg.at[1, rows(0)], own.at[4]),
         pltpu.make_async_copy(blocks, ends, own.at[5]),
     ]
     for copy in own_copies:
@@ -93,12 +94,13 @@
 
     def y_queries(d):
         for a, ref in enumerate((q, g)):
-            go(remote(cols(ref, y_of(d)), qg.at[a, rows(y)], y_send.at[a + 2, d], y_recv.at[a + 2, d], seq_id(x, y_of(d), c)))
+            slot = qg.at[a, rows(SLOT_OF[4 - d])]
+            go(remote(cols(ref, y_of(d)), slot, y_send.at[a + 2, d], y_recv.at[a + 2, d], seq_id(x, y_of(d), c)))
 
     def onward(d):
         there = kv.at[chunk(x, y_of(d), c)]
-        go(remote(there, there, x_send.at[d], x_recv.at[d], x_peer))
-        go(remote(there, there, c_send.at[0, d], c_recv.at[0, d], c_peer))
+        remote(there, there, x_send.at[d], x_recv.at[d], x_peer).start()
+        remote(there, there, c_send.at[0, d], c_recv.at[0, d], c_peer).start()
 
     y_keys(1)
     y_keys(3)
@@ -109,29 +111,41 @@
     y_queries(3)
     y_keys(2)
     y_queries(2)
-    for d in (3, 1, 2):
+    def keys_arrived(d):
         for a in range(2):
             arrived(kv.at[chunk(x, y_of(d), c), a], y_recv.at[a, 4 - d])
         onward(d)
+
+    def queries_arrived(d):
+        for a in range(2):
+            arrived(qg.at[a, rows(SLOT_OF[d])], y_recv.at[a + 2, 4 - d])
+
+    def far_arrived(d):
+        far = kv.at[chunk(1 - x, y_of(d), c)]
+        arrived(far, x_recv.at[d])
+        remote(far, far, c_send.at[1, d], c_recv.at[1, d], c_peer).start()
+
     for copy in own_copies[2:]:
         copy.wait()
-    for d in (3, 1, 2):
-        for a in range(2):
-            arrived(qg.at[a, rows(y_of(d))], y_recv.at[a + 2, 4 - d])
-    for d in range(4):
-        arrived(kv.at[chunk(x, y_of(d), 1 - c)], c_recv.at[0, d])
+    keys_arrived(3)
+    keys_arrived(1)
+    far_arrived(0)
+    queries_arrived(3)
+    queries_arrived(1)
 
     end0 = ends[0]
     end1 = end0 + ends[1]
     lane = lax.broadcasted_iota(jnp.int32, (1, QUERIES), 1)
-    lane_block = 16 * x + 2 * c + 4 * (lane >> 8) + ((lane >> 7) & 1)
+    slot = lane >> 8
+    lane_y = (y + jnp.where(slot == 3, 2, jnp.where(slot == 2, 3, slot))) & 3
+    lane_block = 16 * x + 2 * c + 4 * lane_y + ((lane >> 7) & 1)
     lane_seg = (lane_block >= end0).astype(jnp.int32) + (lane_block >= end1).astype(jnp.int32)
     stats[0] = jnp.full((1, QUERIES), MASKED, F32)
     stats[1] = jnp.zeros((1, QUERIES), F32)
     stats[2] = jnp.zeros((1, QUERIES), F32)
 
-    def pass_a(t):
-        for i in range(4):
+    def pass_a(t, slots):
+        for i in slots:
             sl = slice(i * ROWS, (i + 1) * ROWS)
             s = lax.dot_general(kv[t, 0], qg[0, sl], NT, preferred_element_type=F32)
             d = lax.dot_general(kv[t, 1], qg[1, sl], NT, preferred_element_type=F32)
@@ -157,24 +171,49 @@
             stats[0, :, sl], stats[1, :, sl], stats[2, :, sl] = new, l, r
             m_hist[t, :, sl] = new
 
-    def a_near(n, carry):
-        d = n + n // 2 - 2 * (n // 3)
-        pass_a(chunk(x, y_of(d), c))
-        far = kv.at[chunk(1 - x, y_of(d), c)]
-        arrived(far, x_recv.at[d])
-        remote(far, far, c_send.at[1, d], c_recv.at[1, d], c_peer).start()
-        pass_a(chunk(x, y_of(d), 1 - c))
-        return carry
-
-    def a_far(n, carry):
-        d = n + n // 2 - 2 * (n // 3)
-        pass_a(chunk(1 - x, y_of(d), c))
-        arrived(kv.at[chunk(1 - x, y_of(d), 1 - c)], c_recv.at[1, d])
-        pass_a(chunk(1 - x, y_of(d), 1 - c))
-        return carry
-
-    lax.fori_loop(0, 4, a_near, 0)
-    lax.fori_loop(0, 4, a_far, 0)
+    def half_of(far):
+        return x + far * (1 - 2 * x)
+
+    def early(n):
+        far = n // 3
+        return far, (n + n // 2) * (1 - far)
+
+    def a_first(n, carry):
+        @pl.when(n == 2)
+        def _():
+            keys_arrived(2)
+
+        far, d = early(n)
+        pass_a(chunk(half_of(far), y_of(d), c), (0, 1, 2))
+        peers_chunk = chunk(half_of(far), y_of(d), 1 - c)
+        arrived(kv.at[peers_chunk], c_recv.at[far, d])
+        pass_a(peers_chunk, (0, 1, 2))
+        return carry
+
+    def a_second(n, carry):
+        far, d = early(n)
+        pass_a(chunk(half_of(far), y_of(d), c), (3,))
+        pass_a(chunk(half_of(far), y_of(d), 1 - c), (3,))
+        return carry
+
+    def a_third(n, carry):
+        @pl.when(n == 2)
+        def _():
+            far_arrived(2)
+
+        far, d = (n + 2) // 3, 2 + n - 3 * (n // 2)
+        pass_a(chunk(half_of(far), y_of(d), c), (0, 1, 2, 3))
+        peers_chunk = chunk(half_of(far), y_of(d), 1 - c)
+        arrived(kv.at[peers_chunk], c_recv.at[far, d])
+        pass_a(peers_chunk, (0, 1, 2, 3))
+        return carry
+
+    lax.fori_loop(0, 4, a_first, 0)
+    far_arrived(3)
+    queries_arrived(2)
+    lax.fori_loop(0, 4, a_second, 0)
+    far_arrived(1)
+    lax.fori_loop(0, 4, a_third, 0)
 
     inv = 1.0 / stats[1]
     stats[2] = stats[2] * inv
@@ -253,27 +292,25 @@
     for i in range(4):
         dq_low[i * ROWS : (i + 1) * ROWS] = (dq_acc[:, i * ROWS : (i + 1) * ROWS].T * SCALE).astype(BF16)
     for d in (2, 1, 3):
-        y_copy(0, d, dq_low.at[rows(y_of(d))]).start()
-    last = [pltpu.make_async_copy(dq_low.at[rows(y)], cols(dq_out, y), own.at[1])]
-    last[0].start()
+        y_copy(0, d, dq_low.at[rows(SLOT_OF[d])]).start()
+    own_cols = pl.ds(pl.multiple_of(y * HD, HD), HD)
+    dq_out[:, own_cols] = dq_low[:ROWS]
     sum_near(0)
     finish_near(3)
     for a in range(2):
         y_copy(a + 1, 3, final.at[3, a]).start()
     finish_near(0)
     for a in range(2):
-        copy = pltpu.make_async_copy(final.at[0, a], cols(outs[a + 1], y), own.at[2 + a])
-        copy.start()
-        last.append(copy)
+        outs[a + 1][:, own_cols] = final[0, a]
 
     for d in (3, 2, 1):
         for a in range(3):
             arrived(cols(outs[a], y_of(d)), y2_recv.at[a, 4 - d])
-    for copy in last:
-        copy.wait()
     for copy in sends:
         copy.wait_send()
     for d in range(4):
+        sent(kv.at[0], x_send.at[d])
+        sent(kv.at[0], c_send.at[0, d])
         sent(kv.at[0], c_send.at[1, d])
         sent(to_core.at[0, d], c2_send.at[0, d])
         sent(to_core.at[1, d], c2_send.at[1, d])
@@ -283,11 +320,22 @@
             sent(cols(outs[a], y), y2_send.at[a, d])
 
 
+def store_kernel(dq, dk, dv, dq_out, dk_out, dv_out, done):
+    copies = [
+        pltpu.make_async_copy(src, dst, done.at[i])
+        for i, (src, dst) in enumerate(((dq, dq_out), (dk, dk_out), (dv, dv_out)))
+    ]
+    for copy in copies:
+        copy.start()
+    for copy in copies:
+        copy.wait()
+
+
 def local(query, key_rows, value_rows, out_grad, sample_blocks):
     dma = pltpu.SemaphoreType.DMA
     vmem = pltpu.VMEM
     out = jax.ShapeDtypeStruct((ROWS, 4 * HD), BF16)
-    return pl.pallas_call(
+    grads = pl.pallas_call(
         kernel,
         out_shape=(out,) * 3,
         in_specs=[pl.BlockSpec(memory_space=pl.ANY)] * 5,
@@ -316,6 +364,14 @@
         ),
         name="attention_grads",
     )(sample_blocks, query, key_rows, value_rows, out_grad)
+    return pl.pallas_call(
+        store_kernel,
+        out_shape=(out,) * 3,
+        in_specs=[pl.BlockSpec(memory_space=vmem)] * 3,
+        out_specs=(pl.BlockSpec(memory_space=pl.ANY),) * 3,
+        scratch_shapes=[dma((3,))],
+        name="store",
+    )(*grads)
 
 
 def solution(mesh):

time: 54.6 us -> 50.4 us (0.923)
  local copies, waits for them, and re-layouts: 3.46 us -> 0 us
  Pallas kernels: 49.6 us -> 48.8 us
    unnamed x7 -> x0, local copies, waits for them, and re-layouts: 3.46 us -> none
    pallas_call x1, Pallas kernels: 49.6 us -> 46.8 us  [local(): pl.pallas_call(kernel, out_shape=(out,) * 3, in_specs=[pl.BlockSpec(memor...]
    pallas_call x0 -> x1, Pallas kernels: none -> 2.01 us  [local(): pl.pallas_call(store_kernel, out_shape=(out,) * 3, in_specs=[pl.BlockSpec...]
where the time goes in v3:
time: 50.4 us; the launch traced here: 49.5 us
  Pallas kernels  48.8 us (97%)
  between operations  0.64 us (1%)
    pallas_call x1, Pallas kernels, local(): pl.pallas_call(kernel, out_shape=(out,) * 3, in_specs=[pl.BlockSpec(memor...  46.8 us
    pallas_call x1, Pallas kernels, local(): pl.pallas_call(store_kernel, out_shape=(out,) * 3, in_specs=[pl.BlockSpec...  2.01 us

profile of v3, /device:TPU:0, one launch (start us, length us, event | category | flops | bytes accessed | tf_op | source)
XLA Modules:
  0.0 49.5 jit_solution(11162588601828979013)
XLA Ops:
  0.6 46.8 %attention_grads.1 = (bf16[256,512]{1,0:T(8,128)(2,1)}, bf16[256,512]{1,0:T(8,128)(2,1)}, bf16[256,512]{1,0:T(8,128)(2,1)}) custom-call(s32[3]{0:T(128)} %blocks.1, bf16[256,512]{1,0:T(8,128)(2,1)} %q.1, bf16[256,512]{1,0:T(8,128)(2,1)} %k.1, bf16[256,512]{1,0:T(8,128)(2,1)} %v.1, bf16[256,512]{1,0:T(8,128)(2,1)} %g.1), custom_call_target="tpu_custom_call" | custom-call | tf_op jit(solution)/shard_map/attention_grads/pallas_call | solution.py:338
  47.5 2.0 %store.1 = (bf16[256,512]{1,0:T(8,128)(2,1)}, bf16[256,512]{1,0:T(8,128)(2,1)}, bf16[256,512]{1,0:T(8,128)(2,1)}) custom-call(bf16[256,512]{1,0:T(8,128)(2,1)} %get-tuple-element.6.dq, bf16[256,512]{1,0:T(8,128)(2,1)} %get-tuple-element.7.dk, bf16[256,512]{1,0:T(8,128)(2,1)} %get-tuple-element.8.dv), custom_call_target="tpu_custom_call" | custom-call | tf_op jit(solution)/shard_map/store/pallas_call | solution.py:367

commit v4 on v3

--- a/solution.py
+++ b/solution.py
@@ -88,47 +88,59 @@
         copy.start()
         sends.append(copy)
 
-    def y_keys(d):
-        for a, ref in enumerate((k, v)):
-            go(remote(cols(ref, y_of(d)), kv.at[here, a], y_send.at[a, d], y_recv.at[a, d], seq_id(x, y_of(d), c)))
+    def y_keys(a, d):
+        src = cols((k, v)[a], y_of(d))
+        go(remote(src, kv.at[here, a], y_send.at[a, d], y_recv.at[a, d], seq_id(x, y_of(d), c)))
 
     def y_queries(d):
         for a, ref in enumerate((q, g)):
             slot = qg.at[a, rows(SLOT_OF[4 - d])]
             go(remote(cols(ref, y_of(d)), slot, y_send.at[a + 2, d], y_recv.at[a + 2, d], seq_id(x, y_of(d), c)))
 
-    def onward(d):
-        there = kv.at[chunk(x, y_of(d), c)]
-        remote(there, there, x_send.at[d], x_recv.at[d], x_peer).start()
-        remote(there, there, c_send.at[0, d], c_recv.at[0, d], c_peer).start()
-
-    y_keys(1)
-    y_keys(3)
-    for copy in own_copies[:2]:
-        copy.wait()
-    onward(0)
+    def onward(a, d):
+        there = kv.at[chunk(x, y_of(d), c), a]
+        remote(there, there, x_send.at[a, d], x_recv.at[a, d], x_peer).start()
+        remote(there, there, c_send.at[0, a, d], c_recv.at[0, a, d], c_peer).start()
+
+    for a in range(2):
+        for d in (1, 3):
+            y_keys(a, d)
+    for a in range(2):
+        own_copies[a].wait()
+        onward(a, 0)
     y_queries(1)
     y_queries(3)
-    y_keys(2)
+    for a in range(2):
+        y_keys(a, 2)
     y_queries(2)
-    def keys_arrived(d):
-        for a in range(2):
-            arrived(kv.at[chunk(x, y_of(d), c), a], y_recv.at[a, 4 - d])
-        onward(d)
+    def half_of(far):
+        return x + far * (1 - 2 * x)
+
+    def keys_arrived(a, d):
+        arrived(kv.at[chunk(x, y_of(d), c), a], y_recv.at[a, 4 - d])
+        onward(a, d)
 
     def queries_arrived(d):
         for a in range(2):
             arrived(qg.at[a, rows(SLOT_OF[d])], y_recv.at[a + 2, 4 - d])
 
     def far_arrived(d):
-        far = kv.at[chunk(1 - x, y_of(d), c)]
-        arrived(far, x_recv.at[d])
-        remote(far, far, c_send.at[1, d], c_recv.at[1, d], c_peer).start()
+        for a in range(2):
+            far = kv.at[chunk(1 - x, y_of(d), c), a]
+            arrived(far, x_recv.at[a, d])
+            remote(far, far, c_send.at[1, a, d], c_recv.at[1, a, d], c_peer).start()
+
+    def core_arrived(far, d):
+        t = chunk(half_of(far), y_of(d), 1 - c)
+        for a in range(2):
+            arrived(kv.at[t, a], c_recv.at[far, a, d])
+        return t
 
     for copy in own_copies[2:]:
         copy.wait()
-    keys_arrived(3)
-    keys_arrived(1)
+    for a in range(2):
+        for d in (3, 1):
+            keys_arrived(a, d)
     far_arrived(0)
     queries_arrived(3)
     queries_arrived(1)
@@ -171,9 +183,6 @@
             stats[0, :, sl], stats[1, :, sl], stats[2, :, sl] = new, l, r
             m_hist[t, :, sl] = new
 
-    def half_of(far):
-        return x + far * (1 - 2 * x)
-
     def early(n):
         far = n // 3
         return far, (n + n // 2) * (1 - far)
@@ -181,13 +190,12 @@
     def a_first(n, carry):
         @pl.when(n == 2)
         def _():
-            keys_arrived(2)
+            for a in range(2):
+                keys_arrived(a, 2)
 
         far, d = early(n)
         pass_a(chunk(half_of(far), y_of(d), c), (0, 1, 2))
-        peers_chunk = chunk(half_of(far), y_of(d), 1 - c)
-        arrived(kv.at[peers_chunk], c_recv.at[far, d])
-        pass_a(peers_chunk, (0, 1, 2))
+        pass_a(core_arrived(far, d), (0, 1, 2))
         return carry
 
     def a_second(n, carry):
@@ -203,9 +211,7 @@
 
         far, d = (n + 2) // 3, 2 + n - 3 * (n // 2)
         pass_a(chunk(half_of(far), y_of(d), c), (0, 1, 2, 3))
-        peers_chunk = chunk(half_of(far), y_of(d), 1 - c)
-        arrived(kv.at[peers_chunk], c_recv.at[far, d])
-        pass_a(peers_chunk, (0, 1, 2, 3))
+        pass_a(core_arrived(far, d), (0, 1, 2, 3))
         return carry
 
     lax.fori_loop(0, 4, a_first, 0)
@@ -231,57 +237,83 @@
     def core_copy(far, d):
         return remote(to_core.at[far, d], got_core.at[far, d], c2_send.at[far, d], c2_recv.at[far, d], c_peer)
 
-    def x_copy(d):
-        return remote(to_x.at[d], got_x.at[d], x2_send.at[d], x2_recv.at[d], x_peer)
+    def x_copy(a, d):
+        return remote(to_x.at[d, a], got_x.at[d, a], x2_send.at[a, d], x2_recv.at[a, d], x_peer)
 
     def y_copy(a, d, src):
         return remote(src, cols(outs[a], y), y2_send.at[a, d], y2_recv.at[a, d], seq_id(x, y_of(d), c))
 
-    def finish_far(d):
+    def sum_far(d):
         arrived(got_core.at[0, d], c2_recv.at[0, d])
         to_x[d] = (keep[0, d] + got_core[0, d]).astype(BF16)
-        x_copy(d).start()
 
     def sum_near(d):
         arrived(got_core.at[1, d], c2_recv.at[1, d])
         keep[1, d] = keep[1, d] + got_core[1, d]
 
-    def finish_near(d):
-        arrived(got_x.at[d], x2_recv.at[d])
-        total = keep[1, d] + got_x[d].astype(F32)
-        final[d, 0] = (total[0] * SCALE).astype(BF16)
-        final[d, 1] = total[1].astype(BF16)
+    def final_sum(a, d):
+        arrived(got_x.at[d, a], x2_recv.at[a, d])
+        total = keep[1, d, a] + got_x[d, a].astype(F32)
+        return (total if a else total * SCALE).astype(BF16)
+
+    def finish(a, d):
+        final[d, a] = final_sum(a, d)
+        y_copy(a + 1, d, final.at[d, a]).start()
+
+    def distance(n):
+        back = 3 - n
+        return back + back // 2 - 2 * (back // 3)
 
     def b_far(n, carry):
-        d = lax.rem(n + 1, 4)
+        d = distance(n)
         pass_b(chunk(1 - x, y_of(d), 1 - c), to_core.at[0, d])
         core_copy(0, d).start()
 
-        @pl.when(n > 0)
-        def _():
-            finish_far(n)
+        @pl.when(n == 1)
+        def _():
+            sum_far(2)
+            for a in range(2):
+                x_copy(a, 2).start()
+
+        @pl.when(n == 2)
+        def _():
+            sum_far(3)
+            x_copy(0, 3).start()
+
+        @pl.when(n == 3)
+        def _():
+            sum_far(1)
+            x_copy(0, 1).start()
+            x_copy(1, 3).start()
+            x_copy(1, 1).start()
 
         pass_b(chunk(1 - x, y_of(d), c), keep.at[0, d])
         return carry
 
     def b_near(n, carry):
-        d = lax.rem(n + 1, 4)
+        d = distance(n)
         pass_b(chunk(x, y_of(d), 1 - c), to_core.at[1, d])
         core_copy(1, d).start()
 
         @pl.when(n == 0)
         def _():
-            finish_far(0)
-
-        @pl.when(n > 0)
-        def _():
-            sum_near(n)
-
-        @pl.when(n > 1)
-        def _():
-            finish_near(n - 1)
+            sum_far(0)
             for a in range(2):
-                y_copy(a + 1, n - 1, final.at[n - 1, a]).start()
+                x_copy(a, 0).start()
+
+        @pl.when(n == 1)
+        def _():
+            sum_near(2)
+
+        @pl.when(n == 2)
+        def _():
+            sum_near(3)
+            finish(0, 2)
+
+        @pl.when(n == 3)
+        def _():
+            sum_near(1)
+            finish(1, 2)
 
         pass_b(chunk(x, y_of(d), c), keep.at[1, d])
         return carry
@@ -296,12 +328,11 @@
     own_cols = pl.ds(pl.multiple_of(y * HD, HD), HD)
     dq_out[:, own_cols] = dq_low[:ROWS]
     sum_near(0)
-    finish_near(3)
-    for a in range(2):
-        y_copy(a + 1, 3, final.at[3, a]).start()
-    finish_near(0)
-    for a in range(2):
-        outs[a + 1][:, own_cols] = final[0, a]
+    for a in range(2):
+        finish(a, 3)
+        finish(a, 1)
+    for a in range(2):
+        outs[a + 1][:, own_cols] = final_sum(a, 0)
 
     for d in (3, 2, 1):
         for a in range(3):
@@ -309,12 +340,13 @@
     for copy in sends:
         copy.wait_send()
     for d in range(4):
-        sent(kv.at[0], x_send.at[d])
-        sent(kv.at[0], c_send.at[0, d])
-        sent(kv.at[0], c_send.at[1, d])
+        for a in range(2):
+            sent(kv.at[0, 0], x_send.at[a, d])
+            sent(kv.at[0, 0], c_send.at[0, a, d])
+            sent(kv.at[0, 0], c_send.at[1, a, d])
+            sent(to_x.at[d, a], x2_send.at[a, d])
         sent(to_core.at[0, d], c2_send.at[0, d])
         sent(to_core.at[1, d], c2_send.at[1, d])
-        sent(to_x.at[d], x2_send.at[d])
     for d in (1, 2, 3):
         for a in range(3):
             sent(cols(outs[a], y), y2_send.at[a, d])
@@ -356,8 +388,8 @@
             vmem((4, 2, ROWS, HD), BF16),
             vmem((4, 2, ROWS, HD), BF16),
             pltpu.SMEM((3,), jnp.int32),
-            dma((4, 4)), dma((4, 4)), dma((4,)), dma((4,)), dma((2, 4)), dma((2, 4)), dma((6,)),
-            dma((2, 4)), dma((2, 4)), dma((4,)), dma((4,)), dma((3, 4)), dma((3, 4)),
+            dma((4, 4)), dma((4, 4)), dma((2, 4)), dma((2, 4)), dma((2, 2, 4)), dma((2, 2, 4)), dma((6,)),
+            dma((2, 4)), dma((2, 4)), dma((2, 4)), dma((2, 4)), dma((3, 4)), dma((3, 4)),
         ],
         compiler_params=pltpu.CompilerParams(
             collective_id=0, has_side_effects=True, vmem_limit_bytes=60 << 20

time: 50.4 us -> 48.5 us (0.962)
  Pallas kernels: 48.8 us -> 47.1 us
    pallas_call x1, Pallas kernels: 46.8 us -> 45.1 us  [local(): pl.pallas_call(kernel, out_shape=(out,) * 3, in_specs=[pl.BlockSpec(memor...]
where the time goes in v4:
time: 48.5 us; the launch traced here: 47.7 us
  Pallas kernels  47.1 us (97%)
  between operations  0.64 us (1%)
    pallas_call x1, Pallas kernels, local(): pl.pallas_call(kernel, out_shape=(out,) * 3, in_specs=[pl.BlockSpec(memor...  45.1 us
    pallas_call x1, Pallas kernels, local(): pl.pallas_call(store_kernel, out_shape=(out,) * 3, in_specs=[pl.BlockSpec...  2.01 us

profile of v4, /device:TPU:0, one launch (start us, length us, event | category | flops | bytes accessed | tf_op | source)
XLA Modules:
  0.0 47.7 jit_solution(507721669295364222)
XLA Ops:
  0.6 45.1 %attention_grads.1 = (bf16[256,512]{1,0:T(8,128)(2,1)}, bf16[256,512]{1,0:T(8,128)(2,1)}, bf16[256,512]{1,0:T(8,128)(2,1)}) custom-call(s32[3]{0:T(128)} %blocks.1, bf16[256,512]{1,0:T(8,128)(2,1)} %q.1, bf16[256,512]{1,0:T(8,128)(2,1)} %k.1, bf16[256,512]{1,0:T(8,128)(2,1)} %v.1, bf16[256,512]{1,0:T(8,128)(2,1)} %g.1), custom_call_target="tpu_custom_call" | custom-call | tf_op jit(solution)/shard_map/attention_grads/pallas_call | solution.py:370
  45.7 2.0 %store.1 = (bf16[256,512]{1,0:T(8,128)(2,1)}, bf16[256,512]{1,0:T(8,128)(2,1)}, bf16[256,512]{1,0:T(8,128)(2,1)}) custom-call(bf16[256,512]{1,0:T(8,128)(2,1)} %get-tuple-element.6.dq, bf16[256,512]{1,0:T(8,128)(2,1)} %get-tuple-element.7.dk, bf16[256,512]{1,0:T(8,128)(2,1)} %get-tuple-element.8.dv), custom_call_target="tpu_custom_call" | custom-call | tf_op jit(solution)/shard_map/store/pallas_call | solution.py:399

commit v5 on v4

--- a/solution.py
+++ b/solution.py
@@ -65,6 +65,11 @@
     def sent(src, send):
         remote(src, src, send, own.at[0], x_peer).wait_send()
 
+    peers = [x_peer, c_peer] + [seq_id(x, y_of(d), c) for d in (1, 2, 3)]
+    barrier = pltpu.get_barrier_semaphore()
+    for peer in peers:
+        pl.semaphore_signal(barrier, inc=1, device_id=peer, device_id_type=MESH)
+
     here = chunk(x, y, c)
     own_copies = [
         pltpu.make_async_copy(cols(k, y), kv.at[here, 0], own.at[1]),
@@ -76,10 +81,6 @@
     for copy in own_copies:
         copy.start()
 
-    peers = [x_peer, c_peer] + [seq_id(x, y_of(d), c) for d in (1, 2, 3)]
-    barrier = pltpu.get_barrier_semaphore()
-    for peer in peers:
-        pl.semaphore_signal(barrier, inc=1, device_id=peer, device_id_type=MESH)
     pl.semaphore_wait(barrier, len(peers))
 
     sends = []
@@ -142,8 +143,6 @@
         for d in (3, 1):
             keys_arrived(a, d)
     far_arrived(0)
-    queries_arrived(3)
-    queries_arrived(1)
 
     end0 = ends[0]
     end1 = end0 + ends[1]
@@ -187,21 +186,28 @@
         far = n // 3
         return far, (n + n // 2) * (1 - far)
 
+    def a_own(n, carry):
+        far, d = early(n)
+        pass_a(chunk(half_of(far), y_of(d), c), (0,))
+        pass_a(core_arrived(far, d), (0,))
+        return carry
+
     def a_first(n, carry):
-        @pl.when(n == 2)
+        @pl.when(n == 3)
         def _():
             for a in range(2):
                 keys_arrived(a, 2)
 
         far, d = early(n)
-        pass_a(chunk(half_of(far), y_of(d), c), (0, 1, 2))
-        pass_a(core_arrived(far, d), (0, 1, 2))
+        pass_a(chunk(half_of(far), y_of(d), c), (1, 2))
+        pass_a(chunk(half_of(far), y_of(d), 1 - c), (1, 2))
         return carry
 
     def a_second(n, carry):
-        far, d = early(n)
-        pass_a(chunk(half_of(far), y_of(d), c), (3,))
-        pass_a(chunk(half_of(far), y_of(d), 1 - c), (3,))
+        for item in (2 * n, 2 * n + 1):
+            far, d = early(item)
+            for core in (c, 1 - c):
+                pass_a(chunk(half_of(far), y_of(d), core), (3,))
         return carry
 
     def a_third(n, carry):
@@ -214,10 +220,13 @@
         pass_a(core_arrived(far, d), (0, 1, 2, 3))
         return carry
 
+    lax.fori_loop(0, 4, a_own, 0)
+    queries_arrived(3)
+    queries_arrived(1)
     lax.fori_loop(0, 4, a_first, 0)
     far_arrived(3)
     queries_arrived(2)
-    lax.fori_loop(0, 4, a_second, 0)
+    lax.fori_loop(0, 2, a_second, 0)
     far_arrived(1)
     lax.fori_loop(0, 4, a_third, 0)
 

time: 48.5 us -> 47.6 us (0.981)
  Pallas kernels: 47.1 us -> 46.2 us
    pallas_call x1, Pallas kernels: 45.1 us -> 44.2 us  [local(): pl.pallas_call(kernel, out_shape=(out,) * 3, in_specs=[pl.BlockSpec(memor...]
where the time goes in v5:
time: 47.6 us; the launch traced here: 46.8 us
  Pallas kernels  46.2 us (97%)
  between operations  0.64 us (1%)
    pallas_call x1, Pallas kernels, local(): pl.pallas_call(kernel, out_shape=(out,) * 3, in_specs=[pl.BlockSpec(memor...  44.2 us
    pallas_call x1, Pallas kernels, local(): pl.pallas_call(store_kernel, out_shape=(out,) * 3, in_specs=[pl.BlockSpec...  2.01 us

profile of v5, /device:TPU:0, one launch (start us, length us, event | category | flops | bytes accessed | tf_op | source)
XLA Modules:
  0.0 46.8 jit_solution(15539038919089170500)
XLA Ops:
  0.6 44.2 %attention_grads.1 = (bf16[256,512]{1,0:T(8,128)(2,1)}, bf16[256,512]{1,0:T(8,128)(2,1)}, bf16[256,512]{1,0:T(8,128)(2,1)}) custom-call(s32[3]{0:T(128)} %blocks.1, bf16[256,512]{1,0:T(8,128)(2,1)} %q.1, bf16[256,512]{1,0:T(8,128)(2,1)} %k.1, bf16[256,512]{1,0:T(8,128)(2,1)} %v.1, bf16[256,512]{1,0:T(8,128)(2,1)} %g.1), custom_call_target="tpu_custom_call" | custom-call | tf_op jit(solution)/shard_map/attention_grads/pallas_call | solution.py:379
  44.8 2.0 %store.1 = (bf16[256,512]{1,0:T(8,128)(2,1)}, bf16[256,512]{1,0:T(8,128)(2,1)}, bf16[256,512]{1,0:T(8,128)(2,1)}) custom-call(bf16[256,512]{1,0:T(8,128)(2,1)} %get-tuple-element.6.dq, bf16[256,512]{1,0:T(8,128)(2,1)} %get-tuple-element.7.dk, bf16[256,512]{1,0:T(8,128)(2,1)} %get-tuple-element.8.dv), custom_call_target="tpu_custom_call" | custom-call | tf_op jit(solution)/shard_map/store/pallas_call | solution.py:408

commit v6 on v5

--- a/solution.py
+++ b/solution.py
@@ -203,12 +203,10 @@
         pass_a(chunk(half_of(far), y_of(d), 1 - c), (1, 2))
         return carry
 
-    def a_second(n, carry):
-        for item in (2 * n, 2 * n + 1):
-            far, d = early(item)
+    def a_second():
+        for far, d in ((0, 0), (0, 1), (0, 3), (1, 0)):
             for core in (c, 1 - c):
                 pass_a(chunk(half_of(far), y_of(d), core), (3,))
-        return carry
 
     def a_third(n, carry):
         @pl.when(n == 2)
@@ -226,7 +224,7 @@
     lax.fori_loop(0, 4, a_first, 0)
     far_arrived(3)
     queries_arrived(2)
-    lax.fori_loop(0, 2, a_second, 0)
+    a_second()
     far_arrived(1)
     lax.fori_loop(0, 4, a_third, 0)
 

time: 47.6 us -> 47.5 us (level)
  no operation moved by 1% of the time
where the time goes in v6:
time: 47.5 us; the launch traced here: 46.7 us
  Pallas kernels  46.1 us (97%)
  between operations  0.64 us (1%)
    pallas_call x1, Pallas kernels, local(): pl.pallas_call(kernel, out_shape=(out,) * 3, in_specs=[pl.BlockSpec(memor...  44 us
    pallas_call x1, Pallas kernels, local(): pl.pallas_call(store_kernel, out_shape=(out,) * 3, in_specs=[pl.BlockSpec...  2.01 us

profile of v6, /device:TPU:0, one launch (start us, length us, event | category | flops | bytes accessed | tf_op | source)
XLA Modules:
  0.0 46.7 jit_solution(8760966650537929333)
XLA Ops:
  0.6 44.0 %attention_grads.1 = (bf16[256,512]{1,0:T(8,128)(2,1)}, bf16[256,512]{1,0:T(8,128)(2,1)}, bf16[256,512]{1,0:T(8,128)(2,1)}) custom-call(s32[3]{0:T(128)} %blocks.1, bf16[256,512]{1,0:T(8,128)(2,1)} %q.1, bf16[256,512]{1,0:T(8,128)(2,1)} %k.1, bf16[256,512]{1,0:T(8,128)(2,1)} %v.1, bf16[256,512]{1,0:T(8,128)(2,1)} %g.1), custom_call_target="tpu_custom_call" | custom-call | tf_op jit(solution)/shard_map/attention_grads/pallas_call | solution.py:377
  44.7 2.0 %store.1 = (bf16[256,512]{1,0:T(8,128)(2,1)}, bf16[256,512]{1,0:T(8,128)(2,1)}, bf16[256,512]{1,0:T(8,128)(2,1)}) custom-call(bf16[256,512]{1,0:T(8,128)(2,1)} %get-tuple-element.6.dq, bf16[256,512]{1,0:T(8,128)(2,1)} %get-tuple-element.7.dk, bf16[256,512]{1,0:T(8,128)(2,1)} %get-tuple-element.8.dv), custom_call_target="tpu_custom_call" | custom-call | tf_op jit(solution)/shard_map/store/pallas_call | solution.py:406

commit v7 on v6

--- a/solution.py
+++ b/solution.py
@@ -209,7 +209,7 @@
                 pass_a(chunk(half_of(far), y_of(d), core), (3,))
 
     def a_third(n, carry):
-        @pl.when(n == 2)
+        @pl.when(n == 1)
         def _():
             far_arrived(2)
 

time: 47.5 us -> 48.9 us (1.029)
  the two profiles are of different devices: /device:TPU:0 before, /device:TPU:1 now
where the time goes in v7:
time: 48.9 us; the launch traced here: 48.8 us
  Pallas kernels  48.2 us (99%)
  between operations  0.64 us (1%)
    pallas_call x1, Pallas kernels, local(): pl.pallas_call(kernel, out_shape=(out,) * 3, in_specs=[pl.BlockSpec(memor...  46.1 us
    pallas_call x1, Pallas kernels, local(): pl.pallas_call(store_kernel, out_shape=(out,) * 3, in_specs=[pl.BlockSpec...  2.01 us

profile of v7, /device:TPU:1, one launch (start us, length us, event | category | flops | bytes accessed | tf_op | source)
XLA Modules:
  0.0 48.8 jit_solution(11399268041810421981)
XLA Ops:
  0.6 46.1 %attention_grads.1 = (bf16[256,512]{1,0:T(8,128)(2,1)}, bf16[256,512]{1,0:T(8,128)(2,1)}, bf16[256,512]{1,0:T(8,128)(2,1)}) custom-call(s32[3]{0:T(128)} %blocks.1, bf16[256,512]{1,0:T(8,128)(2,1)} %q.1, bf16[256,512]{1,0:T(8,128)(2,1)} %k.1, bf16[256,512]{1,0:T(8,128)(2,1)} %v.1, bf16[256,512]{1,0:T(8,128)(2,1)} %g.1), custom_call_target="tpu_custom_call" | custom-call | tf_op jit(solution)/shard_map/attention_grads/pallas_call | solution.py:377
  46.8 2.0 %store.1 = (bf16[256,512]{1,0:T(8,128)(2,1)}, bf16[256,512]{1,0:T(8,128)(2,1)}, bf16[256,512]{1,0:T(8,128)(2,1)}) custom-call(bf16[256,512]{1,0:T(8,128)(2,1)} %get-tuple-element.6.dq, bf16[256,512]{1,0:T(8,128)(2,1)} %get-tuple-element.7.dk, bf16[256,512]{1,0:T(8,128)(2,1)} %get-tuple-element.8.dv), custom_call_target="tpu_custom_call" | custom-call | tf_op jit(solution)/shard_map/store/pallas_call | solution.py:406
